TPU v7x, 512 devices: a whole 4x4x16 slice. The times are simulated.
512 devices in a mesh: lat: 16 (over z), lon: 32 (over y, x, core).
Axes of the slice: x: 4, y: 4, z: 16, core: 2. Of those that a mesh axis runs over, the one named last changes fastest.
Arguments:
- state: float32 [4, 32, 256, 4096], P(None, None, 'lat', 'lon'), may hold values from -6 to 6
- damping: float32 [32], replicated, may hold values from 0.02 to 0.2
- cutoff: int32 [256], replicated, may hold values from 1 to 2048, as said below
Outputs:
- advanced: float32 [4, 32, 256, 4096], P(None, None, 'lat', 'lon')
Inputs may be any that keep to these rules, and one draw needn't show every extreme that they name: cutoff[j] is 2048 on every row within 45 degrees of the equator and 1 on the two outermost rows.
All inputs are finite; a program needn't handle non-finite values.
Results may differ from a plain program's by a relative error of at most 0.00005.
Values sent between devices are 32-bit elements; how exact they have to be, the bound alone decides.
No kernel may reach another device: no remote copies, remote signals or barrier semaphores. Data moves between devices by JAX's collectives and lax.ppermute only.
A program may use at most 64 MiB of HBM per device.

v0:
```python
import math

import jax
import jax.numpy as jnp
import numpy as np
from jax import lax
from jax.experimental import pallas as pl
from jax.experimental.pallas import tpu as pltpu
from jax.sharding import PartitionSpec as P

COURANT = 0.05
ROWS = 8
LANES = 128


def metrics(rows, nlat):
    angle = math.pi * ((rows.astype(jnp.float32) + 0.5) / nlat - 0.5)
    return jnp.cos(angle), 2.0 * jnp.sin(angle)


def row_tables(first, nlat, damping, cutoff):
    rows = first - 1 + jnp.arange(ROWS + 2)
    cosine, coriolis = metrics(rows, nlat)
    cos_north = metrics(rows + 1, nlat)[0]
    cos_south = metrics(rows - 1, nlat)[0]
    half = 0.5 / cosine
    inside = ((rows >= 0) & (rows < nlat)).astype(jnp.float32)
    own = [
        half,
        cos_north * half,
        cos_south * half,
        coriolis,
        damping[0] * cosine * cosine,
        damping[1] * cosine * cosine,
    ]
    tiles = [jnp.broadcast_to(v[1:-1, None], (ROWS, LANES)) for v in own]
    for at in (0, ROWS + 1):
        for v in (half, cos_north * half, cos_south * half, jnp.ones_like(half)):
            tiles.append(jnp.broadcast_to((v * inside)[at], (ROWS, LANES)))
    rows = rows[1:-1]
    polar = (rows < nlat // 4) | (rows >= nlat - nlat // 4)
    limit = lax.dynamic_slice(cutoff, (first,), (ROWS,))
    limits = [jnp.broadcast_to(v[:, None], (ROWS, LANES)) for v in (limit, polar.astype(jnp.int32))]
    return jnp.stack(tiles), jnp.stack(limits)


def split(values):
    high = values.astype(jnp.bfloat16)
    low = (values - high.astype(jnp.float32)).astype(jnp.bfloat16)
    return high, low


def fourier_tables(blocks):
    nlon = blocks * LANES
    at = np.arange(LANES)
    phase = 2.0 * np.pi * ((at[:, None] * at[None, :]) % LANES) / LANES
    cos, sin = np.cos(phase), np.sin(phase)
    forward = np.block([[cos, -sin], [sin, cos]])
    inverse = np.block([[cos, sin], [-sin, cos]]) / nlon
    turn = 2.0 * np.pi * np.arange(blocks // 2 + 1)[:, None] * at[None, :] / nlon
    twist = np.stack([np.cos(turn), np.sin(turn)]).astype(np.float32)
    twist = np.broadcast_to(twist[:, :, None, :], (2, blocks // 2 + 1, ROWS, LANES))

    def halves(matrix):
        high = matrix.astype(np.float32).astype(jnp.bfloat16)
        low = (matrix - high.astype(np.float64)).astype(np.float32).astype(jnp.bfloat16)
        return np.stack([high, low])

    return np.ascontiguousarray(twist), halves(forward), halves(inverse)


def root(k, n):
    angle = 2.0 * math.pi * k / n
    return math.cos(angle), math.sin(angle)


def real_fft(x):
    n = len(x)
    if n == 2:
        return [(x[0] + x[1], None), (x[0] - x[1], None)]
    even, odd = real_fft(x[0::2]), real_fft(x[1::2])
    half, quarter = n // 2, n // 4
    out = [None] * (half + 1)
    out[0] = (even[0][0] + odd[0][0], None)
    out[half] = (even[0][0] - odd[0][0], None)
    out[quarter] = (even[quarter][0], -odd[quarter][0])
    for k in range(1, quarter):
        c, s = root(k, n)
        re, im = odd[k]
        t_re, t_im = re * c + im * s, im * c - re * s
        out[k] = (even[k][0] + t_re, even[k][1] + t_im)
        out[half - k] = (even[k][0] - t_re, t_im - even[k][1])
    return out


def real_ifft(w):
    half = len(w) - 1
    n, quarter = 2 * half, half // 2
    if n == 2:
        return [w[0][0] + w[1][0], w[0][0] - w[1][0]]
    even, odd = [None] * (quarter + 1), [None] * (quarter + 1)
    even[0] = (w[0][0] + w[half][0], None)
    odd[0] = (w[0][0] - w[half][0], None)
    even[quarter] = (2.0 * w[quarter][0], None)
    odd[quarter] = (-2.0 * w[quarter][1], None)
    for k in range(1, quarter):
        c, s = root(k, n)
        a, b = w[k], w[half - k]
        even[k] = (a[0] + b[0], a[1] - b[1])
        re, im = a[0] - b[0], a[1] + b[1]
        odd[k] = (re * c - im * s, im * c + re * s)
    x = [None] * n
    x[0::2], x[1::2] = real_ifft(even), real_ifft(odd)
    return x


def pack_kernel(blocks, x_ref, z_ref, c_ref, own_ref):
    core = lax.axis_index("lon") % 2
    stride = 8 * ROWS

    def plane(field, level, row):
        return x_ref[pl.ds((field * 2 + level) * ROWS + row, blocks, stride=stride), :]

    for out, end in ((z_ref, core), (c_ref, 1 - core)):
        edge, inner = end * (ROWS - 1), 1 + end * (ROWS - 3)
        for k, (field, row) in enumerate(((0, edge), (1, edge), (3, edge), (2, edge), (2, inner))):
            for level in range(2):
                out[k * 2 + level] = plane(field, level, row)
    for side in range(2):
        for level in range(2):
            own_ref[side * 2 + level] = plane(2, level, side * (ROWS - 1))


def main_kernel(
    blocks,
    x_ref,
    z_ref,
    c_ref,
    own_ref,
    tab_ref,
    limit_ref,
    twist_ref,
    forward_ref,
    inverse_ref,
    out_ref,
    inc_ref,
    div_ref,
    edge_ref,
    wave_ref,
):
    core = lax.axis_index("lon") % 2
    lane = lax.broadcasted_iota(jnp.int32, (ROWS, LANES), 1)
    row = lax.broadcasted_iota(jnp.int32, (ROWS, LANES), 0)
    first_lane, last_lane = lane == 0, lane == LANES - 1
    first_row, last_row = row == 0, row == ROWS - 1

    def east(here, after):
        return pltpu.roll(jnp.where(first_lane, after, here), LANES - 1, axis=1)

    def west(here, before):
        return pltpu.roll(jnp.where(last_lane, before, here), 1, axis=1)

    def north(here, beyond):
        return jnp.where(last_row, beyond, pltpu.roll(here, ROWS - 1, axis=0))

    def south(here, beyond):
        return jnp.where(first_row, beyond, pltpu.roll(here, 1, axis=0))

    wide = lax.broadcasted_iota(jnp.int32, (blocks, LANES), 1)
    for side in range(2):
        from_z = core == side
        half, up, down, inside = (tab_ref[6 + side * 4 + i][:1] for i in range(4))
        for level in range(2):

            def beyond(k):
                other = c_ref[1 - core, k * 2 + level]
                return jnp.where(from_z, z_ref[k * 2 + level], other) * inside

            thick, zonal, potential, near, far = (beyond(k) for k in range(5))
            after = pltpu.roll(zonal, blocks - 1, axis=0)
            before = pltpu.roll(zonal, 1, axis=0)
            after = pltpu.roll(jnp.where(wide == 0, after, zonal), LANES - 1, axis=1)
            before = pltpu.roll(jnp.where(wide == LANES - 1, before, zonal), 1, axis=1)
            own = own_ref[side * 2 + level]
            above, below = (far, own) if side else (own, far)
            div = (after - before) * half + up * above - down * below
            for k, v in enumerate(((1.0 + thick) * near, near, thick, potential, div)):
                edge_ref[side, k * 2 + level] = v

    half, up, down, coriolis = (tab_ref[i] for i in range(4))

    def ends(k, level, p):
        return edge_ref[0, k * 2 + level, pl.ds(p, 1), :], edge_ref[1, k * 2 + level, pl.ds(p, 1), :]

    def divergence(p, carry):
        before, after = lax.rem(p + blocks - 1, blocks), lax.rem(p + 1, blocks)
        for level in range(2):
            u, v = 2 + level, 4 + level
            zonal, merid = x_ref[p, u], x_ref[p, v]
            lo, hi = ends(1, level, p)
            div_ref[p, level] = (
                (east(zonal, x_ref[after, u]) - west(zonal, x_ref[before, u])) * half
                + up * north(merid, hi)
                - down * south(merid, lo)
            )
        return carry

    lax.fori_loop(0, blocks, divergence, 0, unroll=4)

    def increments(p, carry):
        before, after = lax.rem(p + blocks - 1, blocks), lax.rem(p + 1, blocks)
        for level in range(2):
            h, u, v, t = level, 2 + level, 4 + level, 6 + level
            damp = tab_ref[4 + level]
            thick, zonal, merid, potential = x_ref[p, h], x_ref[p, u], x_ref[p, v], x_ref[p, t]
            thick_b, thick_a = x_ref[before, h], x_ref[after, h]
            carried = 1.0 + thick
            flux = carried * zonal
            flux_a = (1.0 + thick_a) * x_ref[after, u]
            flux_b = (1.0 + thick_b) * x_ref[before, u]
            flow = carried * merid
            lo, hi = ends(0, level, p)
            inc_ref[p, h] = -COURANT * (
                (east(flux, flux_a) - west(flux, flux_b)) * half
                + up * north(flow, hi)
                - down * south(flow, lo)
            )
            div = div_ref[p, level]
            slope = (east(thick, thick_a) - west(thick, thick_b)) * half
            spread = (east(div, div_ref[after, level]) - west(div, div_ref[before, level])) * half
            inc_ref[p, u] = COURANT * (coriolis * merid - slope) + damp * spread
            lo, hi = ends(2, level, p)
            slope = (north(thick, hi) - south(thick, lo)) * 0.5
            lo, hi = ends(4, level, p)
            spread = (north(div, hi) - south(div, lo)) * 0.5
            inc_ref[p, v] = COURANT * (-coriolis * zonal - slope) + damp * spread
            slope = (east(potential, x_ref[after, t]) - west(potential, x_ref[before, t])) * half
            lo, hi = ends(3, level, p)
            rise = (north(potential, hi) - south(potential, lo)) * 0.5
            inc_ref[p, t] = -COURANT * (zonal * slope + merid * rise)
        return carry

    lax.fori_loop(0, blocks, increments, 0, unroll=2)

    polar = limit_ref[1]
    top = blocks // 2
    nlon = blocks * LANES

    @pl.when(jnp.max(polar) == 0)
    def _():
        out_ref[...] = x_ref[...] + inc_ref[...]

    @pl.when(jnp.max(polar) > 0)
    def _():
        def analyse(g, carry):
            waves = real_fft([inc_ref[p, g] for p in range(blocks)])
            rows = pl.ds(pl.multiple_of(g * ROWS, ROWS), ROWS)
            for k, (re, im) in enumerate(waves):
                c, s = twist_ref[0, k], twist_ref[1, k]
                if im is None:
                    turned = (re, jnp.zeros_like(re)) if k == 0 else (re * c, -(re * s))
                else:
                    turned = (re * c + im * s, im * c - re * s)
                wave_ref[k, rows, :LANES], wave_ref[k, rows, LANES:] = turned
            return carry

        lax.fori_loop(0, 8, analyse, 0)

        def product(values, table_ref):
            high, low = split(values)
            dot = lambda a, b: jnp.dot(a, b, preferred_element_type=jnp.float32)
            return dot(high, table_ref[0]) + dot(low, table_ref[0]) + dot(high, table_ref[1])

        count = (top + 1) * 8 * ROWS
        spectrum = product(wave_ref[...].reshape(count, 2 * LANES), forward_ref)
        spectrum = spectrum.reshape(top + 1, 8, ROWS, 2 * LANES)
        wave = lax.broadcasted_iota(jnp.int32, (top + 1, 1, ROWS, LANES), 0)
        wave = wave + blocks * lax.broadcasted_iota(jnp.int32, (top + 1, 1, ROWS, LANES), 3)
        kept = jnp.minimum(wave, nlon - wave) <= limit_ref[0]
        kept = jnp.concatenate([kept, kept], axis=-1)
        spectrum = jnp.where(kept, spectrum, 0.0).reshape(count, 2 * LANES)
        wave_ref[...] = product(spectrum, inverse_ref).reshape(top + 1, 8 * ROWS, 2 * LANES)

        def rebuild(g, carry):
            rows = pl.ds(pl.multiple_of(g * ROWS, ROWS), ROWS)
            waves = []
            for k in range(top + 1):
                re, im = wave_ref[k, rows, :LANES], wave_ref[k, rows, LANES:]
                c, s = twist_ref[0, k], twist_ref[1, k]
                if k == 0:
                    waves.append((re, None))
                elif k == top:
                    waves.append((re * c - im * s, None))
                else:
                    waves.append((re * c - im * s, im * c + re * s))
            for p, smooth in enumerate(real_ifft(waves)):
                out_ref[p, g] = x_ref[p, g] + jnp.where(polar > 0, smooth, inc_ref[p, g])
            return carry

        lax.fori_loop(0, 8, rebuild, 0)


def on_device(state, damping, cutoff):
    fields, levels, nrow, ncol = state.shape
    nlat = nrow * lax.axis_size("lat")
    blocks = lax.axis_size("lon")
    bands = lax.axis_size("lat")
    lat, lon = lax.axis_index("lat"), lax.axis_index("lon")
    core = lon % 2
    chips = blocks // 2

    parts = state.reshape(fields, chips, 2, 2, ROWS, ncol).transpose(1, 3, 0, 2, 4, 5)
    parts = parts.reshape(blocks, fields * 2, ROWS, ncol)
    circles = lax.all_to_all(parts, "lon", split_axis=0, concat_axis=0, tiled=True)

    first = lat * nrow + core * ROWS
    damp = lax.dynamic_slice(damping, (lon // 2 * 2,), (2,))
    tables, limits = row_tables(first, nlat, damp, cutoff)
    twist, forward, inverse = fourier_tables(blocks)

    vmem = pl.BlockSpec(memory_space=pltpu.VMEM)
    params = pltpu.CompilerParams(vmem_limit_bytes=40 * 2**20)
    plane = jax.ShapeDtypeStruct((10, blocks, ncol), jnp.float32)
    z_mine, c_mine, own = pl.pallas_call(
        lambda *refs: pack_kernel(blocks, *refs),
        out_shape=(plane, plane, jax.ShapeDtypeStruct((4, blocks, ncol), jnp.float32)),
        in_specs=[vmem],
        out_specs=(vmem, vmem, vmem),
        compiler_params=params,
        name="pack",
    )(circles.reshape(-1, ncol))

    swaps = []
    for z in range(bands):
        for m in range(chips):
            a, b = z * blocks + 2 * m + 1, (z + 1) % bands * blocks + 2 * m
            swaps += [(a, b), (b, a)]
    z_other = lax.ppermute(z_mine, ("lat", "lon"), swaps)
    pairs = [[2 * m, 2 * m + 1] for m in range(chips)]
    c_both = lax.all_gather(c_mine, "lon", axis_index_groups=pairs)

    moved = pl.pallas_call(
        lambda *refs: main_kernel(blocks, *refs),
        out_shape=jax.ShapeDtypeStruct(circles.shape, jnp.float32),
        in_specs=[vmem] * 9,
        out_specs=vmem,
        scratch_shapes=[
            pltpu.VMEM(circles.shape, jnp.float32),
            pltpu.VMEM((blocks, 2, ROWS, ncol), jnp.float32),
            pltpu.VMEM((2, 10, blocks, ncol), jnp.float32),
            pltpu.VMEM((blocks // 2 + 1, 8 * ROWS, 2 * ncol), jnp.float32),
        ],
        compiler_params=params,
        name="substep",
    )(circles, z_other, c_both, own, tables, limits, twist, forward, inverse)

    home = lax.all_to_all(moved, "lon", split_axis=0, concat_axis=0, tiled=True)
    home = home.reshape(chips, 2, fields, 2, ROWS, ncol).transpose(2, 0, 3, 1, 4, 5)
    return home.reshape(state.shape)


def solution(mesh):
    in_specs = (P(None, None, "lat", "lon"), P(), P())
    out_specs = P(None, None, "lat", "lon")
    return jax.shard_map(
        on_device, mesh=mesh, in_specs=in_specs, out_specs=out_specs, check_vma=False
    )
```

profile of v0, /device:TPU:1, one launch (start us, length us, event | category | flops | bytes accessed | tf_op | source)
XLA Modules:
  0.0 70.3 jit_solution(11314426265863902928)
XLA Ops:
  0.0 2.3 %copy.9 = f32[4,16,2,2,8,128]{5,4,2,0,3,1:T(8,128)} copy(f32[4,16,2,2,8,128]{5,4,3,2,1,0:T(8,128)} %bitcast.23) | data formatting | bytes 2097152 | tf_op jit(solution)/shard_map/reshape | solution.py:312
  2.3 10.5 %all-to-all-start = ((f32[32,8,8,128]{3,2,1,0:T(8,128)}), f32[32,8,8,128]{3,2,1,0:T(8,128)S(1)}, u32[]{:S(2)}, u32[]{:S(2)}) async-start(f32[32,8,8,128]{3,2,1,0:T(8,128)} %bitcast.2), calls=%async_computation | async-start | bytes 2097152 | tf_op jit(solution)/shard_map/all_to_all | solution.py:314
  13.1 0.1 slice.51
  13.2 0.7 copy-done.4
  13.8 0.1 dynamic_slice.6
  13.9 0.6 fusion.6
  14.5 1.3 %multiply_multiply_fusion = (f32[10]{0:T(128)S(1)}, f32[10]{0:T(128)S(1)}) fusion(f32[]{:T(128)} %bitcast.6, s32[]{:T(128)S(6)} %sub.19, f32[]{:T(128)} %bitcast.5), kind=kLoop, calls=%fused_computation.17 | loop fusion | flops 100 | bytes 92 | tf_op jit(solution)/shard_map/mul | solution.py:34
  15.8 0.1 slice.58
  15.8 0.1 slice.56
  16.0 0.6 fusion.3
  16.6 0.7 fusion.4
  17.4 0.6 fusion.5
  18.4 0.6 constant_dynamic-update-slice_fusion.7
  19.0 0.6 constant_dynamic-update-slice_fusion.6
  19.7 0.7 copy-done.3
  20.4 0.1 dynamic_slice.7
  20.4 0.7 constant_dynamic-update-slice_fusion.5
  21.1 0.7 fusion.2
  21.8 0.6 constant_dynamic-update-slice_fusion.4
  22.4 0.6 constant_dynamic-update-slice_fusion.3
  23.0 0.7 constant_dynamic-update-slice_fusion.2
  23.7 0.5 constant_dynamic-update-slice_fusion.1
  24.2 0.1 or_convert_fusion
  24.3 0.1 stack_broadcast_in_dim.79
  24.5 5.6 %all-to-all-done.refs_0_ = f32[32,8,8,128]{3,2,1,0:T(8,128)S(1)} async-done(((f32[32,8,8,128]{3,2,1,0:T(8,128)}), f32[32,8,8,128]{3,2,1,0:T(8,128)S(1)}, u32[]{:S(2)}, u32[]{:S(2)}) %all-to-all-start) | async-done | bytes 1048608 | tf_op jit(solution)/shard_map/all_to_all | solution.py:314
  30.1 0.2 pack.1
  30.3 2.1 %collective-permute-start = (f32[10,32,128]{2,1,0:T(8,128)S(1)}, f32[10,32,128]{2,1,0:T(8,128)S(1)}, u32[]{:S(2)}, u32[]{:S(2)}) collective-permute-start(f32[10,32,128]{2,1,0:T(8,128)S(1)} %get-tuple-element.8), channel_id=1, source_target_pairs={{1,32},{32,1},{3,34},{34,3},{5,36},{36,5},{7,38},{38,7},{9,40},{40... | collective-permute-start | bytes 491528 | tf_op jit(solution)/shard_map/ppermute | solution.py:338
  32.4 0.7 constant_dynamic-update-slice_fusion.refs_4_
  33.1 9.4 %all-gather = f32[20,32,128]{2,1,0:T(8,128)S(1)} all-gather(f32[10,32,128]{2,1,0:T(8,128)S(1)} %get-tuple-element.9), channel_id=2, replica_groups={{0,1},{2,3},{4,5},{6,7},{8,9},{10,11},{12,13},{14,15},{16,17},{18,19},{..., dimensions={0}, use_global_device_ids=true | all-gather | bytes 491520 | tf_op jit(solution)/shard_map/all_gather | solution.py:340
  42.5 5.6 %substep.1 = f32[32,8,8,128]{3,2,1,0:T(8,128)S(1)} custom-call(f32[32,8,8,128]{3,2,1,0:T(8,128)S(1)} %all-to-all-done.refs_0_, f32[10,32,128]{2,1,0:T(8,128)S(1)} %collective-permute-done.refs_1_, f32[2,10,32,128]{3,2,1,0:T(8,128)S(1)} %bitcast.21, f32[4,32,128]{2,1,0:T(8,128)S(1)} %get-tuple-element.10.refs_3_, ...), custom_call_target="tpu_custom_call" | custom-call | tf_op jit(solution)/shard_map/substep/pallas_call | solution.py:342
  48.2 21.0 %all_to_all.10 = f32[32,8,8,128]{3,2,1,0:T(8,128)S(1)} all-to-all(f32[32,8,8,128]{3,2,1,0:T(8,128)S(1)} %substep.1), channel_id=1, replica_groups=mesh['lat'=16,'lon'=32] {'lon'}, dimensions={0} | all-to-all | bytes 2097152 | tf_op jit(solution)/shard_map/all_to_all | solution.py:357
  69.2 1.1 %copy.10 = f32[4,16,2,2,8,128]{5,4,3,2,1,0:T(8,128)} copy(f32[4,16,2,2,8,128]{5,4,2,0,3,1:T(8,128)S(1)} %bitcast.22) | data formatting | bytes 2097152 | tf_op jit(solution)/shard_map/transpose | solution.py:358
  (26 shorter events, 1.0 us)
Async XLA Ops:
  2.3 27.8 %all-to-all-start = ((f32[32,8,8,128]{3,2,1,0:T(8,128)}), f32[32,8,8,128]{3,2,1,0:T(8,128)S(1)}, u32[]{:S(2)}, u32[]{:S(2)}) async-start(f32[32,8,8,128]{3,2,1,0:T(8,128)} %bitcast.2), calls=%async_computation | async-start | bytes 2097152 | tf_op jit(solution)/shard_map/all_to_all | solution.py:314
  13.2 0.7 copy-start.4
  19.7 0.7 copy-start.3
  30.1 12.4 %copy-start.1 = (bf16[2,256,256]{2,1,0:T(8,128)(2,1)S(1)}, bf16[2,256,256]{2,1,0:T(8,128)(2,1)}, u32[]{:S(2)}) copy-start(bf16[2,256,256]{2,1,0:T(8,128)(2,1)} %constant.78.clone.refs_7_) | copy-start | bytes 786436
  30.3 12.2 %copy-start = (bf16[2,256,256]{2,1,0:T(8,128)(2,1)S(1)}, bf16[2,256,256]{2,1,0:T(8,128)(2,1)}, u32[]{:S(2)}) copy-start(bf16[2,256,256]{2,1,0:T(8,128)(2,1)} %constant.79.clone.refs_8_) | copy-start | bytes 786436
  30.3 12.2 %collective-permute-start = (f32[10,32,128]{2,1,0:T(8,128)S(1)}, f32[10,32,128]{2,1,0:T(8,128)S(1)}, u32[]{:S(2)}, u32[]{:S(2)}) collective-permute-start(f32[10,32,128]{2,1,0:T(8,128)S(1)} %get-tuple-element.8), channel_id=1, source_target_pairs={{1,32},{32,1},{3,34},{34,3},{5,36},{36,5},{7,38},{38,7},{9,40},{40... | collective-permute-start | bytes 491528 | tf_op jit(solution)/shard_map/ppermute | solution.py:338
  33.1 9.4 %copy-start.2 = (f32[2,17,8,128]{3,2,1,0:T(8,128)S(1)}, f32[2,17,8,128]{3,2,1,0:T(8,128)}, u32[]{:S(2)}) copy-start(f32[2,17,8,128]{3,2,1,0:T(8,128)} %constant.77.clone.refs_6_) | copy-start | bytes 417796
where the time goes:
time: 70.8 us; the launch traced here: 70.3 us
  blocking collectives  30.5 us (43%)
  local copies, waits for them, and re-layouts  14.1 us (20%)
  starting transfers between devices  12.5 us (18%)
  Pallas kernels  5.86 us (8%)
  waiting for transfers between devices  5.62 us (8%)
  other arithmetic  1.6 us (2%)
    all_to_all x1, blocking collectives, on_device(): home = lax.all_to_all(moved, 'lon', split_axis=0, concat_axis=0, tiled=True)  21 us
    all_to_all x1, starting transfers between devices, on_device(): lax.all_to_all(parts, 'lon', split_axis=0, concat_axis=0, tiled=True)  10.5 us
    all_gather x1, blocking collectives, on_device(): c_both = lax.all_gather(c_mine, 'lon', axis_index_groups=pairs)  9.42 us
    unnamed x23, local copies, waits for them, and re-layouts  6.12 us
    pallas_call x1, Pallas kernels, on_device(): pl.pallas_call(lambda *refs: main_kernel(blocks, *refs), out_shape=jax.Sh...  5.62 us
    all_to_all x1, waiting for transfers between devices, on_device(): lax.all_to_all(parts, 'lon', split_axis=0, concat_axis=0, tiled=True)  5.62 us
    slice x4, local copies, waits for them, and re-layouts, row_tables(): tiles.append(jnp.broadcast_to((v * inside)[at], (ROWS, LANES)))  2.5 us
    reshape x1, local copies, waits for them, and re-layouts, on_device(): state.reshape(fields, chips, 2, 2, ROWS, ncol).transpose(1, 3, 0, 2, 4, 5)  2.33 us
  transfers between devices with their start and end apart: 2, of which 1 were waited for; matrix products, arithmetic and copies ran while one was open for 15% of the time, Pallas kernels for 0%

commit v1 on v0

v1 whole, which is shorter than its diff:
```python
import math

import jax
import jax.numpy as jnp
import numpy as np
from jax import lax
from jax.experimental import pallas as pl
from jax.experimental.pallas import tpu as pltpu
from jax.sharding import PartitionSpec as P

COURANT = 0.05
ROWS = 8
LANES = 128


def row_constants(nlat):
    rows = np.arange(-2, nlat + 2)
    angle = np.float32(math.pi) * ((rows.astype(np.float32) + np.float32(0.5)) / np.float32(nlat) - np.float32(0.5))
    cosine, sine = np.cos(angle.astype(np.float64)), np.sin(angle.astype(np.float64))
    half = 0.5 / cosine[1:-1]
    up, down = cosine[2:] * half, cosine[:-2] * half
    inside = (rows[1:-1] >= 0) & (rows[1:-1] < nlat)
    first, last = np.arange(nlat) % ROWS == 0, np.arange(nlat) % ROWS == ROWS - 1
    own = slice(1, -1)
    polar = (np.arange(nlat) < nlat // 4) | (np.arange(nlat) >= nlat - nlat // 4)
    tiles = [
        half[own],
        np.where(last, 0.0, up[own]),
        np.where(first, 0.0, down[own]),
        2.0 * sine[2:-2],
        cosine[2:-2] ** 2,
        np.where(last, 0.0, 0.5),
        np.where(first, 0.0, 0.5),
        up[own],
        down[own],
        polar.astype(np.float64),
    ]
    tiles = [t.reshape(-1, ROWS) for t in tiles]
    for at in (0, ROWS + 1):
        for v in (half, up, down, np.ones_like(half)):
            edge = (v * inside)[at : at + nlat : ROWS][: nlat // ROWS]
            tiles.append(np.broadcast_to(edge[:, None], (nlat // ROWS, ROWS)))
    table = np.stack(tiles, 1).astype(np.float32)
    return np.ascontiguousarray(np.broadcast_to(table[..., None], table.shape + (LANES,)))


def split(values):
    high = values.astype(jnp.bfloat16)
    low = (values - high.astype(jnp.float32)).astype(jnp.bfloat16)
    return high, low


def fourier_tables(blocks):
    nlon = blocks * LANES
    at = np.arange(LANES)
    phase = 2.0 * np.pi * ((at[:, None] * at[None, :]) % LANES) / LANES
    cos, sin = np.cos(phase), np.sin(phase)
    forward = np.block([[cos, -sin], [sin, cos]])
    inverse = np.block([[cos, sin], [-sin, cos]]) / nlon
    turn = 2.0 * np.pi * np.arange(blocks // 2 + 1)[:, None] * at[None, :] / nlon
    twist = np.stack([np.cos(turn), np.sin(turn)]).astype(np.float32)
    twist = np.broadcast_to(twist[:, :, None, :], (2, blocks // 2 + 1, ROWS, LANES))

    def halves(matrix):
        high = matrix.astype(np.float32).astype(jnp.bfloat16)
        low = (matrix - high.astype(np.float64)).astype(np.float32).astype(jnp.bfloat16)
        return np.stack([high, low])

    return np.ascontiguousarray(twist), halves(forward), halves(inverse)


def root(k, n):
    angle = 2.0 * math.pi * k / n
    return math.cos(angle), math.sin(angle)


def real_fft(x):
    n = len(x)
    if n == 2:
        return [(x[0] + x[1], None), (x[0] - x[1], None)]
    even, odd = real_fft(x[0::2]), real_fft(x[1::2])
    half, quarter = n // 2, n // 4
    out = [None] * (half + 1)
    out[0] = (even[0][0] + odd[0][0], None)
    out[half] = (even[0][0] - odd[0][0], None)
    out[quarter] = (even[quarter][0], -odd[quarter][0])
    for k in range(1, quarter):
        c, s = root(k, n)
        re, im = odd[k]
        t_re, t_im = re * c + im * s, im * c - re * s
        out[k] = (even[k][0] + t_re, even[k][1] + t_im)
        out[half - k] = (even[k][0] - t_re, t_im - even[k][1])
    return out


def real_ifft(w):
    half = len(w) - 1
    n, quarter = 2 * half, half // 2
    if n == 2:
        return [w[0][0] + w[1][0], w[0][0] - w[1][0]]
    even, odd = [None] * (quarter + 1), [None] * (quarter + 1)
    even[0] = (w[0][0] + w[half][0], None)
    odd[0] = (w[0][0] - w[half][0], None)
    even[quarter] = (2.0 * w[quarter][0], None)
    odd[quarter] = (-2.0 * w[quarter][1], None)
    for k in range(1, quarter):
        c, s = root(k, n)
        a, b = w[k], w[half - k]
        even[k] = (a[0] + b[0], a[1] - b[1])
        re, im = a[0] - b[0], a[1] + b[1]
        odd[k] = (re * c - im * s, im * c + re * s)
    x = [None] * n
    x[0::2], x[1::2] = real_ifft(even), real_ifft(odd)
    return x


def spread_kernel(x_ref, out_ref, sems):
    copies = []
    for field in range(4):
        for core in range(2):
            copies.append(
                pltpu.make_async_copy(
                    x_ref.at[field, :, :, core], out_ref.at[:, core, field], sems.at[field, core]
                )
            )
    for copy in copies:
        copy.start()
    for copy in copies:
        copy.wait()


def collect_kernel(x_ref, out_ref, sems):
    copies = []
    for field in range(4):
        for core in range(2):
            copies.append(
                pltpu.make_async_copy(
                    x_ref.at[:, core, field], out_ref.at[field, :, :, core], sems.at[field, core]
                )
            )
    for copy in copies:
        copy.start()
    for copy in copies:
        copy.wait()


def pack_kernel(blocks, x_ref, z_ref, c_ref, own_ref):
    core = lax.axis_index("lon") % 2

    def plane(field, level, row):
        return x_ref[pl.ds((field * 2 + level) * ROWS + row, blocks, stride=8 * ROWS), :]

    for out, end in ((z_ref, core), (c_ref, 1 - core)):
        edge, inner = end * (ROWS - 1), 1 + end * (ROWS - 3)
        for k, (field, row) in enumerate(((0, edge), (1, edge), (3, edge), (2, edge), (2, inner))):
            for level in range(2):
                out[k * 2 + level] = plane(field, level, row)
    for side in range(2):
        for level in range(2):
            own_ref[side * 2 + level] = plane(2, level, side * (ROWS - 1))


def tile(p, g):
    return pl.ds(pl.multiple_of((p * 8 + g) * ROWS, ROWS), ROWS)


def stencil_kernel(blocks, x_ref, tab_ref, damp_ref, inc_ref, div_ref):
    lane = lax.broadcasted_iota(jnp.int32, (ROWS, LANES), 1)
    first_lane, last_lane = lane == 0, lane == LANES - 1

    def zonal_diff(before, here, after):
        east = pltpu.roll(jnp.where(first_lane, after, here), LANES - 1, axis=1)
        west = pltpu.roll(jnp.where(last_lane, before, here), 1, axis=1)
        return (east - west) * tab_ref[0]

    def north(here):
        return pltpu.roll(here, ROWS - 1, axis=0)

    def south(here):
        return pltpu.roll(here, 1, axis=0)

    def merid_flux(here):
        return tab_ref[1] * north(here) - tab_ref[2] * south(here)

    def merid_diff(here):
        return tab_ref[5] * north(here) - tab_ref[6] * south(here)

    def x(p, g):
        return x_ref[tile(p, g), :]

    def around(p):
        return lax.rem(p + blocks - 1, blocks), lax.rem(p + 1, blocks)

    def divergence(p, carry):
        before, after = around(p)
        for level in range(2):
            u, v = 2 + level, 4 + level
            div_ref[p, level] = zonal_diff(x(before, u), x(p, u), x(after, u)) + merid_flux(x(p, v))
        return carry

    lax.fori_loop(0, blocks, divergence, 0, unroll=4)

    def increments(p, carry):
        before, after = around(p)
        for level in range(2):
            h, u, v, t = level, 2 + level, 4 + level, 6 + level
            damp = tab_ref[4] * damp_ref[level]
            thick, zonal, merid, potential = x(p, h), x(p, u), x(p, v), x(p, t)
            thick_b, thick_a = x(before, h), x(after, h)
            carried = 1.0 + thick
            flux_b, flux_a = (1.0 + thick_b) * x(before, u), (1.0 + thick_a) * x(after, u)
            inc_ref[tile(p, h), :] = -COURANT * (
                zonal_diff(flux_b, carried * zonal, flux_a) + merid_flux(carried * merid)
            )
            div = div_ref[p, level]
            inc_ref[tile(p, u), :] = COURANT * (
                tab_ref[3] * merid - zonal_diff(thick_b, thick, thick_a)
            ) + damp * zonal_diff(div_ref[before, level], div, div_ref[after, level])
            inc_ref[tile(p, v), :] = damp * merid_diff(div) - COURANT * (
                tab_ref[3] * zonal + merid_diff(thick)
            )
            inc_ref[tile(p, t), :] = -COURANT * (
                zonal * zonal_diff(x(before, t), potential, x(after, t))
                + merid * merid_diff(potential)
            )
        return carry

    lax.fori_loop(0, blocks, increments, 0, unroll=2)


def filter_kernel(
    blocks,
    x_ref,
    inc_ref,
    z_ref,
    c_ref,
    own_ref,
    tab_ref,
    damp_ref,
    limit_ref,
    twist_ref,
    forward_ref,
    inverse_ref,
    out_ref,
    wave_ref,
):
    del inc_ref
    core = lax.axis_index("lon") % 2
    lane = lax.broadcasted_iota(jnp.int32, (blocks, LANES), 1)

    def shifted_diff(v):
        after = jnp.where(lane == 0, pltpu.roll(v, blocks - 1, axis=0), v)
        before = jnp.where(lane == LANES - 1, pltpu.roll(v, 1, axis=0), v)
        return pltpu.roll(after, LANES - 1, axis=1) - pltpu.roll(before, 1, axis=1)

    def add(group, row, value):
        rows = pl.ds(group * ROWS + row, blocks, stride=8 * ROWS)
        out_ref[rows, :] = out_ref[rows, :] + value

    for side in range(2):
        edge, inner = side * (ROWS - 1), 1 + side * (ROWS - 3)
        half, up, down, inside = (tab_ref[10 + side * 4 + i, :1] for i in range(4))
        weight = tab_ref[8 - side, edge : edge + 1] * (1.0 if side else -1.0)
        step = 0.5 if side else -0.5
        for level in range(2):
            damp = tab_ref[4] * damp_ref[level]
            damp_edge, damp_inner = damp[edge : edge + 1], damp[inner : inner + 1]

            def beyond(k):
                other = c_ref[1 - core, k * 2 + level]
                return jnp.where(core == side, z_ref[k * 2 + level], other) * inside

            thick, zonal, potential, near, far = (beyond(k) for k in range(5))
            own = own_ref[side * 2 + level]
            above, below = (far, own) if side else (own, far)
            div = shifted_diff(zonal) * half + up * above - down * below
            more = weight * near
            add(level, edge, -COURANT * weight * ((1.0 + thick) * near))
            add(2 + level, edge, damp_edge * tab_ref[0, edge : edge + 1] * shifted_diff(more))
            add(4 + level, edge, step * (damp_edge * div - COURANT * thick))
            add(4 + level, inner, step * damp_inner * more)
            add(6 + level, edge, -COURANT * step * (own * potential))

    polar = tab_ref[9]
    top = blocks // 2
    nlon = blocks * LANES

    @pl.when(jnp.max(polar) == 0)
    def _():
        out_ref[...] = x_ref[...] + out_ref[...]

    @pl.when(jnp.max(polar) > 0)
    def _():
        def analyse(g, carry):
            waves = real_fft([out_ref[tile(p, g), :] for p in range(blocks)])
            rows = pl.ds(pl.multiple_of(g * ROWS, ROWS), ROWS)
            for k, (re, im) in enumerate(waves):
                c, s = twist_ref[0, k], twist_ref[1, k]
                if im is None:
                    turned = (re, jnp.zeros_like(re)) if k == 0 else (re * c, -(re * s))
                else:
                    turned = (re * c + im * s, im * c - re * s)
                wave_ref[k, rows, :LANES], wave_ref[k, rows, LANES:] = turned
            return carry

        lax.fori_loop(0, 8, analyse, 0)

        def product(values, table_ref):
            high, low = split(values)
            dot = lambda a, b: jnp.dot(a, b, preferred_element_type=jnp.float32)
            return dot(high, table_ref[0]) + dot(low, table_ref[0]) + dot(high, table_ref[1])

        count = (top + 1) * 8 * ROWS
        spectrum = product(wave_ref[...].reshape(count, 2 * LANES), forward_ref)
        spectrum = spectrum.reshape(top + 1, 8, ROWS, 2 * LANES)
        wave = lax.broadcasted_iota(jnp.int32, (top + 1, 1, ROWS, LANES), 0)
        wave = wave + blocks * lax.broadcasted_iota(jnp.int32, (top + 1, 1, ROWS, LANES), 3)
        kept = jnp.minimum(wave, nlon - wave) <= limit_ref[...]
        kept = jnp.concatenate([kept, kept], axis=-1)
        spectrum = jnp.where(kept, spectrum, 0.0).reshape(count, 2 * LANES)
        wave_ref[...] = product(spectrum, inverse_ref).reshape(top + 1, 8 * ROWS, 2 * LANES)

        def rebuild(g, carry):
            rows = pl.ds(pl.multiple_of(g * ROWS, ROWS), ROWS)
            waves = []
            for k in range(top + 1):
                re, im = wave_ref[k, rows, :LANES], wave_ref[k, rows, LANES:]
                c, s = twist_ref[0, k], twist_ref[1, k]
                if k == 0:
                    waves.append((re, None))
                elif k == top:
                    waves.append((re * c - im * s, None))
                else:
                    waves.append((re * c - im * s, im * c + re * s))
            for p, smooth in enumerate(real_ifft(waves)):
                at = tile(p, g)
                out_ref[at, :] = x_ref[at, :] + jnp.where(polar > 0, smooth, out_ref[at, :])
            return carry

        lax.fori_loop(0, 8, rebuild, 0)


def on_device(state, damping, cutoff):
    fields, levels, nrow, ncol = state.shape
    bands, blocks = lax.axis_size("lat"), lax.axis_size("lon")
    lat, lon = lax.axis_index("lat"), lax.axis_index("lon")
    chips = blocks // 2
    vmem, hbm = pl.BlockSpec(memory_space=pltpu.VMEM), pl.BlockSpec(memory_space=pltpu.HBM)
    params = pltpu.CompilerParams(vmem_limit_bytes=40 * 2**20)

    def call(kernel, name, out, ins, outs, cost, scratch=(), aliases=None):
        return pl.pallas_call(
            kernel,
            out_shape=out,
            in_specs=ins,
            out_specs=outs,
            scratch_shapes=scratch,
            compiler_params=params,
            input_output_aliases=aliases or {},
            cost_estimate=pl.CostEstimate(flops=cost, bytes_accessed=2**22, transcendentals=0),
            name=name,
        )

    def array(*shape):
        return jax.ShapeDtypeStruct(shape, jnp.float32)

    sems = [pltpu.SemaphoreType.DMA((fields, 2))]
    parts = call(
        spread_kernel, "spread", array(chips, 2, fields, 2, ROWS, ncol), [hbm], vmem, 0, sems
    )(state.reshape(fields, chips, 2, 2, ROWS, ncol))
    circles = lax.all_to_all(
        parts.reshape(blocks, -1, ncol), "lon", split_axis=0, concat_axis=0, tiled=True
    ).reshape(-1, ncol)

    group = lat * (nrow // ROWS) + lon % 2
    tables = lax.dynamic_index_in_dim(row_constants(nrow * bands), group, keepdims=False)
    damp = lax.dynamic_slice(damping, (lon // 2 * 2,), (2,))
    damp = jnp.broadcast_to(damp[:, None, None], (2, ROWS, ncol))
    limit = lax.dynamic_slice(cutoff, (group * ROWS,), (ROWS,))
    limit = jnp.broadcast_to(limit[:, None], (ROWS, ncol))
    twist, forward, inverse = fourier_tables(blocks)

    plane = array(10, blocks, ncol)
    z_mine, c_mine, own = call(
        lambda *refs: pack_kernel(blocks, *refs),
        "pack",
        (plane, plane, array(4, blocks, ncol)),
        [vmem],
        (vmem, vmem, vmem),
        0,
    )(circles)

    swaps = []
    for z in range(bands - 1):
        for m in range(chips):
            a, b = z * blocks + 2 * m + 1, (z + 1) * blocks + 2 * m
            swaps += [(a, b), (b, a)]
    z_other = lax.ppermute(z_mine, ("lat", "lon"), swaps)
    pairs = [[2 * m, 2 * m + 1] for m in range(chips)]
    c_both = lax.all_gather(c_mine, "lon", axis_index_groups=pairs)
    increments = call(
        lambda *refs: stencil_kernel(blocks, *refs),
        "stencil",
        array(*circles.shape),
        [vmem] * 3,
        vmem,
        2**31,
        [pltpu.VMEM((blocks, 2, ROWS, ncol), jnp.float32)],
    )(circles, tables, damp)
    moved = call(
        lambda *refs: filter_kernel(blocks, *refs),
        "filter",
        array(*circles.shape),
        [vmem] * 11,
        vmem,
        2**31,
        [pltpu.VMEM((blocks // 2 + 1, 8 * ROWS, 2 * ncol), jnp.float32)],
        {1: 0},
    )(circles, increments, z_other, c_both, own, tables, damp, limit, twist, forward, inverse)

    home = lax.all_to_all(
        moved.reshape(blocks, -1, ncol), "lon", split_axis=0, concat_axis=0, tiled=True
    )
    out = call(
        collect_kernel, "collect", array(fields, chips, 2, 2, ROWS, ncol), [vmem], hbm, 0, sems
    )(home.reshape(chips, 2, fields, 2, ROWS, ncol))
    return out.reshape(state.shape)


def solution(mesh):
    in_specs = (P(None, None, "lat", "lon"), P(), P())
    out_specs = P(None, None, "lat", "lon")
    return jax.shard_map(
        on_device, mesh=mesh, in_specs=in_specs, out_specs=out_specs, check_vma=False
    )
```

time: 70.8 us -> 62.4 us (0.88)
  local copies, waits for them, and re-layouts: 14.1 us -> 2.45 us
  waiting for transfers between devices: 5.62 us -> 16.3 us
  blocking collectives: 30.5 us -> 22.7 us
  Pallas kernels: 5.86 us -> 8.2 us
  other arithmetic: 1.6 us -> 0 us
    all_to_all x1, waiting for transfers between devices: 5.62 us -> 16.2 us  [on_device(): lax.all_to_all(parts.reshape(blocks, -1, ncol), 'lon', split_axis=0, conc...]
    all_gather x1, blocking collectives: 9.42 us -> 2.04 us  [on_device(): c_both = lax.all_gather(c_mine, 'lon', axis_index_groups=pairs)]
    unnamed x23 -> x12, local copies, waits for them, and re-layouts: 6.12 us -> 1.27 us
    slice x11 -> x0, local copies, waits for them, and re-layouts: 3.52 us -> none  [the longest x4 2.5 us: row_tables(): tiles.append(jnp.broadcast_to((v * inside)[at], (ROWS, LANES)))]
    pallas_call x2 -> x5, Pallas kernels: 5.86 us -> 8.2 us  [the longest x1 3.32 us: on_device(): call(lambda *refs: filter_kernel(blocks, *refs), 'filter', array(*circles...]
    reshape x1 -> x0, local copies, waits for them, and re-layouts: 2.33 us -> none  [on_device(): state.reshape(fields, chips, 2, 2, ROWS, ncol).transpose(1, 3, 0, 2, 4, 5)]
    mul x4 -> x0, other arithmetic: 1.46 us -> none  [the longest x1 1.28 us: row_tables(): damping[1] * cosine * cosine]
    transpose x1 -> x0, local copies, waits for them, and re-layouts: 1.11 us -> none  [on_device(): home.reshape(chips, 2, fields, 2, ROWS, ncol).transpose(2, 0, 3, 1, 4, 5)]
  transfers between devices with their start and end apart: 2 -> 2, of which waited for: 1 -> 2; matrix products, arithmetic and copies ran while one was open for 15% -> 2% of each run, Pallas kernels for 0% -> 4%
where the time goes in v1:
time: 62.4 us; the launch traced here: 62.1 us
  blocking collectives  22.7 us (36%)
  waiting for transfers between devices  16.3 us (26%)
  starting transfers between devices  12.4 us (20%)
  Pallas kernels  8.2 us (13%)
  local copies, waits for them, and re-layouts  2.45 us (4%)
    all_to_all x1, blocking collectives, on_device(): lax.all_to_all(moved.reshape(blocks, -1, ncol), 'lon', split_axis=0, conc...  20.6 us
    all_to_all x1, waiting for transfers between devices, on_device(): lax.all_to_all(parts.reshape(blocks, -1, ncol), 'lon', split_axis=0, conc...  16.2 us
    all_to_all x1, starting transfers between devices, on_device(): lax.all_to_all(parts.reshape(blocks, -1, ncol), 'lon', split_axis=0, conc...  10.5 us
    pallas_call x1, Pallas kernels, on_device(): call(lambda *refs: filter_kernel(blocks, *refs), 'filter', array(*circles...  3.32 us
    pallas_call x1, Pallas kernels, on_device(): call(lambda *refs: stencil_kernel(blocks, *refs), 'stencil', array(*circl...  2.49 us
    all_gather x1, blocking collectives, on_device(): c_both = lax.all_gather(c_mine, 'lon', axis_index_groups=pairs)  2.04 us
    ppermute x1, starting transfers between devices, on_device(): z_other = lax.ppermute(z_mine, ('lat', 'lon'), swaps)  1.92 us
    unnamed x12, local copies, waits for them, and re-layouts  1.27 us
  transfers between devices with their start and end apart: 2, of which 2 were waited for; matrix products, arithmetic and copies ran while one was open for 2% of the time, Pallas kernels for 4%

profile of v1, /device:TPU:1, one launch (start us, length us, event | category | flops | bytes accessed | tf_op | source)
XLA Modules:
  0.0 62.1 jit_solution(407522953270821418)
XLA Ops:
  0.0 0.0 copy-start.4
  0.0 0.0 copy-start.5
  0.0 0.0 copy-start
  0.0 1.2 %copy-done = f32[4,32,16,128]{3,2,1,0:T(8,128)S(1)} copy-done((f32[4,32,16,128]{3,2,1,0:T(8,128)S(1)}, f32[4,32,16,128]{3,2,1,0:T(8,128)}, u32[]{:S(2)}) %copy-start) | copy-done | bytes 1048600
  1.3 1.1 %spread.1 = f32[16,2,4,2,8,128]{5,4,3,2,1,0:T(8,128)} custom-call(f32[4,16,2,2,8,128]{5,4,3,2,1,0:T(8,128)S(1)} %bitcast.13), custom_call_target="tpu_custom_call" | custom-call | bytes 4194304 | tf_op jit(solution)/shard_map/spread/pallas_call | solution.py:368
  2.4 10.5 %all-to-all-start = ((f32[32,64,128]{2,1,0:T(8,128)}), f32[32,64,128]{2,1,0:T(8,128)S(1)}, u32[]{:S(2)}, u32[]{:S(2)}) async-start(f32[32,64,128]{2,1,0:T(8,128)} %bitcast.1), calls=%async_computation | async-start | bytes 2097152 | tf_op jit(solution)/shard_map/all_to_all | solution.py:371
  12.9 0.0 copy-done.4
  12.9 0.1 dynamic_slice.12
  13.0 0.0 copy-done.5
  13.0 0.1 dynamic_slice.11
  13.1 0.9 %dynamic-slice_bitcast_fusion.refs_1_.refs_5_ = f32[18,8,128]{2,1,0:T(8,128)S(1)} fusion(f32[32,18,8,128]{3,2,1,0:T(8,128)} %constant.52.clone, s32[]{:T(128)S(6)} %select_n.22), kind=kLoop, calls=%fused_computation | loop fusion | bytes 147460 | tf_op jit(solution)/shard_map/jit(dynamic_index_in_dim)/squeeze | solution.py:376
  14.0 16.2 %all-to-all-done = f32[32,64,128]{2,1,0:T(8,128)S(1)} async-done(((f32[32,64,128]{2,1,0:T(8,128)}), f32[32,64,128]{2,1,0:T(8,128)S(1)}, u32[]{:S(2)}, u32[]{:S(2)}) %all-to-all-start) | async-done | bytes 1048608 | tf_op jit(solution)/shard_map/all_to_all | solution.py:371
  30.2 0.2 pack.1
  30.4 1.9 %collective-permute-start = (f32[10,32,128]{2,1,0:T(8,128)S(1)}, f32[10,32,128]{2,1,0:T(8,128)S(1)}, u32[]{:S(2)}, u32[]{:S(2)}) collective-permute-start(f32[10,32,128]{2,1,0:T(8,128)S(1)} %get-tuple-element.8), channel_id=1, source_target_pairs={{1,32},{32,1},{3,34},{34,3},{5,36},{36,5},{7,38},{38,7},{9,40},{40... | collective-permute-start | bytes 491528 | tf_op jit(solution)/shard_map/ppermute | solution.py:398
  32.3 2.0 %all-gather = f32[20,32,128]{2,1,0:T(8,128)S(1)} all-gather(f32[10,32,128]{2,1,0:T(8,128)S(1)} %get-tuple-element.9), channel_id=2, replica_groups={{0,1},{2,3},{4,5},{6,7},{8,9},{10,11},{12,13},{14,15},{16,17},{18,19},{..., dimensions={0}, use_global_device_ids=true | all-gather | bytes 491520 | tf_op jit(solution)/shard_map/all_gather | solution.py:400
  34.4 0.1 broadcast_in_dim.4.refs_2_.refs_6_
  34.4 0.0 copy-start.1
  34.4 0.0 copy-start.2
  34.4 0.0 copy-start.3
  34.4 2.5 %stencil.1.refs_1_ = f32[2048,128]{1,0:T(8,128)S(1)} custom-call(f32[2048,128]{1,0:T(8,128)S(1)} %bitcast.10, f32[18,8,128]{2,1,0:T(8,128)S(1)} %dynamic-slice_bitcast_fusion.refs_1_.refs_5_, f32[2,8,128]{2,1,0:T(8,128)S(1)} %broadcast_in_dim.4.refs_2_.refs_6_), custom_call_target="tpu_custom_call" | custom-call | flops 2147483648 | bytes 4194304 | tf_op jit(solution)/shard_map/stencil/pallas_call | solution.py:401
  36.9 0.1 collective-permute-done.refs_2_
  37.0 0.1 broadcast_in_dim.5.refs_7_
  37.1 0.0 copy-done.1
  37.1 0.0 copy-done.2
  37.1 0.0 copy-done.3
  37.1 3.3 %filter.1 = f32[2048,128]{1,0:T(8,128)S(1)} custom-call(f32[2048,128]{1,0:T(8,128)S(1)} %bitcast.11, f32[2048,128]{1,0:T(8,128)S(1)} %stencil.1.refs_1_, f32[10,32,128]{2,1,0:T(8,128)S(1)} %collective-permute-done.refs_2_, f32[2,10,32,128]{3,2,1,0:T(8,128)S(1)} %bitcast.15, ...), custom_call_target="tpu_custom_call", output_to_operand_aliasing={{}: (1, {})} | custom-call | flops 2147483648 | bytes 4194304 | tf_op jit(solution)/shard_map/filter/pallas_call | solution.py:410
  40.4 20.6 %all_to_all.10 = f32[32,64,128]{2,1,0:T(8,128)S(1)} all-to-all(f32[32,64,128]{2,1,0:T(8,128)S(1)} %bitcast.14), channel_id=1, replica_groups=mesh['lat'=16,'lon'=32] {'lon'}, dimensions={0} | all-to-all | bytes 2097152 | tf_op jit(solution)/shard_map/all_to_all | solution.py:421
  61.1 1.0 %collect.1 = f32[4,16,2,2,8,128]{5,4,3,2,1,0:T(8,128)} custom-call(f32[16,2,4,2,8,128]{5,4,3,2,1,0:T(8,128)S(1)} %bitcast.12), custom_call_target="tpu_custom_call" | custom-call | bytes 4194304 | tf_op jit(solution)/shard_map/collect/pallas_call | solution.py:424
Async XLA Ops:
  0.0 12.9 %copy-start.4 = (s32[256]{0:T(256)S(1)}, s32[256]{0:T(256)}, u32[]{:S(2)}) copy-start(s32[256]{0:T(256)} %param.9) | copy-start | bytes 3076
  0.0 13.0 %copy-start.5 = (f32[32]{0:T(128)S(1)}, f32[32]{0:T(128)}, u32[]{:S(2)}) copy-start(f32[32]{0:T(128)} %param.8) | copy-start | bytes 388
  0.0 1.3 %copy-start = (f32[4,32,16,128]{3,2,1,0:T(8,128)S(1)}, f32[4,32,16,128]{3,2,1,0:T(8,128)}, u32[]{:S(2)}) copy-start(f32[4,32,16,128]{3,2,1,0:T(8,128)} %param.7) | copy-start | bytes 3145732
  2.4 27.8 %all-to-all-start = ((f32[32,64,128]{2,1,0:T(8,128)}), f32[32,64,128]{2,1,0:T(8,128)S(1)}, u32[]{:S(2)}, u32[]{:S(2)}) async-start(f32[32,64,128]{2,1,0:T(8,128)} %bitcast.1), calls=%async_computation | async-start | bytes 2097152 | tf_op jit(solution)/shard_map/all_to_all | solution.py:371
  30.4 6.6 %collective-permute-start = (f32[10,32,128]{2,1,0:T(8,128)S(1)}, f32[10,32,128]{2,1,0:T(8,128)S(1)}, u32[]{:S(2)}, u32[]{:S(2)}) collective-permute-start(f32[10,32,128]{2,1,0:T(8,128)S(1)} %get-tuple-element.8), channel_id=1, source_target_pairs={{1,32},{32,1},{3,34},{34,3},{5,36},{36,5},{7,38},{38,7},{9,40},{40... | collective-permute-start | bytes 491528 | tf_op jit(solution)/shard_map/ppermute | solution.py:398
  34.4 2.7 %copy-start.1 = (bf16[2,256,256]{2,1,0:T(8,128)(2,1)S(1)}, bf16[2,256,256]{2,1,0:T(8,128)(2,1)}, u32[]{:S(2)}) copy-start(bf16[2,256,256]{2,1,0:T(8,128)(2,1)} %constant.55.clone.refs_10_) | copy-start | bytes 786436
  34.4 2.7 %copy-start.2 = (bf16[2,256,256]{2,1,0:T(8,128)(2,1)S(1)}, bf16[2,256,256]{2,1,0:T(8,128)(2,1)}, u32[]{:S(2)}) copy-start(bf16[2,256,256]{2,1,0:T(8,128)(2,1)} %constant.54.clone.refs_9_) | copy-start | bytes 786436
  34.4 2.7 %copy-start.3 = (f32[2,17,8,128]{3,2,1,0:T(8,128)S(1)}, f32[2,17,8,128]{3,2,1,0:T(8,128)}, u32[]{:S(2)}) copy-start(f32[2,17,8,128]{3,2,1,0:T(8,128)} %constant.53.clone.refs_8_) | copy-start | bytes 417796

commit v2 on v1

--- a/solution.py
+++ b/solution.py
@@ -13,35 +13,41 @@
 LANES = 128
 
 
-def row_constants(nlat):
-    rows = np.arange(-2, nlat + 2)
-    angle = np.float32(math.pi) * ((rows.astype(np.float32) + np.float32(0.5)) / np.float32(nlat) - np.float32(0.5))
-    cosine, sine = np.cos(angle.astype(np.float64)), np.sin(angle.astype(np.float64))
-    half = 0.5 / cosine[1:-1]
-    up, down = cosine[2:] * half, cosine[:-2] * half
-    inside = (rows[1:-1] >= 0) & (rows[1:-1] < nlat)
-    first, last = np.arange(nlat) % ROWS == 0, np.arange(nlat) % ROWS == ROWS - 1
-    own = slice(1, -1)
-    polar = (np.arange(nlat) < nlat // 4) | (np.arange(nlat) >= nlat - nlat // 4)
-    tiles = [
-        half[own],
-        np.where(last, 0.0, up[own]),
-        np.where(first, 0.0, down[own]),
-        2.0 * sine[2:-2],
-        cosine[2:-2] ** 2,
-        np.where(last, 0.0, 0.5),
-        np.where(first, 0.0, 0.5),
-        up[own],
-        down[own],
-        polar.astype(np.float64),
-    ]
-    tiles = [t.reshape(-1, ROWS) for t in tiles]
-    for at in (0, ROWS + 1):
-        for v in (half, up, down, np.ones_like(half)):
-            edge = (v * inside)[at : at + nlat : ROWS][: nlat // ROWS]
-            tiles.append(np.broadcast_to(edge[:, None], (nlat // ROWS, ROWS)))
-    table = np.stack(tiles, 1).astype(np.float32)
-    return np.ascontiguousarray(np.broadcast_to(table[..., None], table.shape + (LANES,)))
+def sine(angle):
+    square = angle * angle
+    total = jnp.zeros_like(angle)
+    for n in (13, 11, 9, 7, 5, 3, 1):
+        total = total * square + (-1.0) ** (n // 2) / math.factorial(n)
+    return total * angle
+
+
+class Rows:
+    def __init__(self, bands):
+        self.core = lax.axis_index("lon") % 2
+        self.first = (lax.axis_index("lat") * 2 + self.core) * ROWS
+        self.nlat = nlat = bands * 2 * ROWS
+        row = lax.broadcasted_iota(jnp.int32, (ROWS, LANES), 0)
+        near = self.first + row
+        at = self.cosine(near)
+        self.half = 0.5 / at
+        self.up, self.down = self.cosine(near + 1) * self.half, self.cosine(near - 1) * self.half
+        middle = near.astype(jnp.float32) + (0.5 - 0.5 * nlat)
+        self.coriolis = 2.0 * sine(middle * (math.pi / nlat))
+        self.square = at * at
+        self.polar = (near < nlat // 4) | (near >= nlat - nlat // 4)
+        ends = self.first + jnp.where(row < 3, row - 2, row + ROWS - 4)
+        self.ends = self.cosine(ends)
+
+    def cosine(self, row):
+        index = row.astype(jnp.float32) + 0.5
+        return sine(jnp.minimum(index, self.nlat - index) * (math.pi / self.nlat))
+
+    def beside(self, side):
+        below, at, above = (self.ends[side * 3 + i : side * 3 + i + 1] for i in range(3))
+        row = self.first + (ROWS if side else -1)
+        inside = ((row >= 0) & (row < self.nlat)).astype(jnp.float32)
+        half = 0.5 / at * inside
+        return half, above * half, below * half, inside
 
 
 def split(values):
@@ -160,18 +166,41 @@
             own_ref[side * 2 + level] = plane(2, level, side * (ROWS - 1))
 
 
+def parameters(rows, damp_ref, cutoff_ref, param_ref):
+    level = lax.axis_index("lon") // 2 * 2
+    damping = damp_ref[...].reshape(1, -1)
+    at = lax.broadcasted_iota(jnp.int32, damping.shape, 1)
+    for i in range(2):
+        one = jnp.sum(jnp.where(at == level + i, damping, 0.0), axis=1, keepdims=True)
+        param_ref[i] = jnp.broadcast_to(one, (ROWS, LANES))
+    cutoff = cutoff_ref[...].astype(jnp.float32).reshape(1, -1)
+    cutoff = jnp.broadcast_to(cutoff, (ROWS, cutoff.shape[1]))
+    at = lax.broadcasted_iota(jnp.int32, cutoff.shape, 1)
+    row = lax.broadcasted_iota(jnp.int32, cutoff.shape, 0)
+    limit = jnp.sum(jnp.where(at == rows.first + row, cutoff, 0.0), axis=1, keepdims=True)
+    param_ref[2] = jnp.broadcast_to(limit, (ROWS, LANES))
+
+
 def tile(p, g):
     return pl.ds(pl.multiple_of((p * 8 + g) * ROWS, ROWS), ROWS)
 
 
-def stencil_kernel(blocks, x_ref, tab_ref, damp_ref, inc_ref, div_ref):
+def stencil_kernel(bands, blocks, x_ref, damp_ref, cutoff_ref, inc_ref, param_ref, div_ref):
+    rows = Rows(bands)
+    parameters(rows, damp_ref, cutoff_ref, param_ref)
+    row = lax.broadcasted_iota(jnp.int32, (ROWS, LANES), 0)
+    up = jnp.where(row == ROWS - 1, 0.0, rows.up)
+    down = jnp.where(row == 0, 0.0, rows.down)
+    half_up = jnp.where(row == ROWS - 1, 0.0, 0.5)
+    half_down = jnp.where(row == 0, 0.0, 0.5)
+    damping = [rows.square * param_ref[i] for i in range(2)]
     lane = lax.broadcasted_iota(jnp.int32, (ROWS, LANES), 1)
     first_lane, last_lane = lane == 0, lane == LANES - 1
 
     def zonal_diff(before, here, after):
         east = pltpu.roll(jnp.where(first_lane, after, here), LANES - 1, axis=1)
         west = pltpu.roll(jnp.where(last_lane, before, here), 1, axis=1)
-        return (east - west) * tab_ref[0]
+        return (east - west) * rows.half
 
     def north(here):
         return pltpu.roll(here, ROWS - 1, axis=0)
@@ -180,10 +209,10 @@
         return pltpu.roll(here, 1, axis=0)
 
     def merid_flux(here):
-        return tab_ref[1] * north(here) - tab_ref[2] * south(here)
+        return up * north(here) - down * south(here)
 
     def merid_diff(here):
-        return tab_ref[5] * north(here) - tab_ref[6] * south(here)
+        return half_up * north(here) - half_down * south(here)
 
     def x(p, g):
         return x_ref[tile(p, g), :]
@@ -204,7 +233,7 @@
         before, after = around(p)
         for level in range(2):
             h, u, v, t = level, 2 + level, 4 + level, 6 + level
-            damp = tab_ref[4] * damp_ref[level]
+            damp = damping[level]
             thick, zonal, merid, potential = x(p, h), x(p, u), x(p, v), x(p, t)
             thick_b, thick_a = x(before, h), x(after, h)
             carried = 1.0 + thick
@@ -214,10 +243,10 @@
             )
             div = div_ref[p, level]
             inc_ref[tile(p, u), :] = COURANT * (
-                tab_ref[3] * merid - zonal_diff(thick_b, thick, thick_a)
+                rows.coriolis * merid - zonal_diff(thick_b, thick, thick_a)
             ) + damp * zonal_diff(div_ref[before, level], div, div_ref[after, level])
             inc_ref[tile(p, v), :] = damp * merid_diff(div) - COURANT * (
-                tab_ref[3] * zonal + merid_diff(thick)
+                rows.coriolis * zonal + merid_diff(thick)
             )
             inc_ref[tile(p, t), :] = -COURANT * (
                 zonal * zonal_diff(x(before, t), potential, x(after, t))
@@ -229,15 +258,14 @@
 
 
 def filter_kernel(
+    bands,
     blocks,
     x_ref,
     inc_ref,
     z_ref,
     c_ref,
     own_ref,
-    tab_ref,
-    damp_ref,
-    limit_ref,
+    param_ref,
     twist_ref,
     forward_ref,
     inverse_ref,
@@ -245,7 +273,8 @@
     wave_ref,
 ):
     del inc_ref
-    core = lax.axis_index("lon") % 2
+    rows = Rows(bands)
+    damping = [rows.square * param_ref[i] for i in range(2)]
     lane = lax.broadcasted_iota(jnp.int32, (blocks, LANES), 1)
 
     def shifted_diff(v):
@@ -254,21 +283,21 @@
         return pltpu.roll(after, LANES - 1, axis=1) - pltpu.roll(before, 1, axis=1)
 
     def add(group, row, value):
-        rows = pl.ds(group * ROWS + row, blocks, stride=8 * ROWS)
-        out_ref[rows, :] = out_ref[rows, :] + value
+        at = pl.ds(group * ROWS + row, blocks, stride=8 * ROWS)
+        out_ref[at, :] = out_ref[at, :] + value
 
     for side in range(2):
         edge, inner = side * (ROWS - 1), 1 + side * (ROWS - 3)
-        half, up, down, inside = (tab_ref[10 + side * 4 + i, :1] for i in range(4))
-        weight = tab_ref[8 - side, edge : edge + 1] * (1.0 if side else -1.0)
+        half, up, down, inside = rows.beside(side)
+        weight = rows.up[edge : edge + 1] if side else -rows.down[edge : edge + 1]
         step = 0.5 if side else -0.5
         for level in range(2):
-            damp = tab_ref[4] * damp_ref[level]
+            damp = damping[level]
             damp_edge, damp_inner = damp[edge : edge + 1], damp[inner : inner + 1]
 
             def beyond(k):
-                other = c_ref[1 - core, k * 2 + level]
-                return jnp.where(core == side, z_ref[k * 2 + level], other) * inside
+                other = c_ref[1 - rows.core, k * 2 + level]
+                return jnp.where(rows.core == side, z_ref[k * 2 + level], other) * inside
 
             thick, zonal, potential, near, far = (beyond(k) for k in range(5))
             own = own_ref[side * 2 + level]
@@ -276,31 +305,33 @@
             div = shifted_diff(zonal) * half + up * above - down * below
             more = weight * near
             add(level, edge, -COURANT * weight * ((1.0 + thick) * near))
-            add(2 + level, edge, damp_edge * tab_ref[0, edge : edge + 1] * shifted_diff(more))
+            add(2 + level, edge, damp_edge * rows.half[edge : edge + 1] * shifted_diff(more))
             add(4 + level, edge, step * (damp_edge * div - COURANT * thick))
             add(4 + level, inner, step * damp_inner * more)
             add(6 + level, edge, -COURANT * step * (own * potential))
 
-    polar = tab_ref[9]
+    polar = rows.polar
+    limit = param_ref[2].astype(jnp.int32)
+    any_polar = (rows.first < rows.nlat // 4) | (rows.first + ROWS > rows.nlat - rows.nlat // 4)
     top = blocks // 2
     nlon = blocks * LANES
 
-    @pl.when(jnp.max(polar) == 0)
+    @pl.when(jnp.logical_not(any_polar))
     def _():
         out_ref[...] = x_ref[...] + out_ref[...]
 
-    @pl.when(jnp.max(polar) > 0)
+    @pl.when(any_polar)
     def _():
         def analyse(g, carry):
             waves = real_fft([out_ref[tile(p, g), :] for p in range(blocks)])
-            rows = pl.ds(pl.multiple_of(g * ROWS, ROWS), ROWS)
+            at = pl.ds(pl.multiple_of(g * ROWS, ROWS), ROWS)
             for k, (re, im) in enumerate(waves):
                 c, s = twist_ref[0, k], twist_ref[1, k]
                 if im is None:
                     turned = (re, jnp.zeros_like(re)) if k == 0 else (re * c, -(re * s))
                 else:
                     turned = (re * c + im * s, im * c - re * s)
-                wave_ref[k, rows, :LANES], wave_ref[k, rows, LANES:] = turned
+                wave_ref[k, at, :LANES], wave_ref[k, at, LANES:] = turned
             return carry
 
         lax.fori_loop(0, 8, analyse, 0)
@@ -315,16 +346,16 @@
         spectrum = spectrum.reshape(top + 1, 8, ROWS, 2 * LANES)
         wave = lax.broadcasted_iota(jnp.int32, (top + 1, 1, ROWS, LANES), 0)
         wave = wave + blocks * lax.broadcasted_iota(jnp.int32, (top + 1, 1, ROWS, LANES), 3)
-        kept = jnp.minimum(wave, nlon - wave) <= limit_ref[...]
+        kept = jnp.minimum(wave, nlon - wave) <= limit
         kept = jnp.concatenate([kept, kept], axis=-1)
         spectrum = jnp.where(kept, spectrum, 0.0).reshape(count, 2 * LANES)
         wave_ref[...] = product(spectrum, inverse_ref).reshape(top + 1, 8 * ROWS, 2 * LANES)
 
         def rebuild(g, carry):
-            rows = pl.ds(pl.multiple_of(g * ROWS, ROWS), ROWS)
+            at = pl.ds(pl.multiple_of(g * ROWS, ROWS), ROWS)
             waves = []
             for k in range(top + 1):
-                re, im = wave_ref[k, rows, :LANES], wave_ref[k, rows, LANES:]
+                re, im = wave_ref[k, at, :LANES], wave_ref[k, at, LANES:]
                 c, s = twist_ref[0, k], twist_ref[1, k]
                 if k == 0:
                     waves.append((re, None))
@@ -333,8 +364,8 @@
                 else:
                     waves.append((re * c - im * s, im * c + re * s))
             for p, smooth in enumerate(real_ifft(waves)):
-                at = tile(p, g)
-                out_ref[at, :] = x_ref[at, :] + jnp.where(polar > 0, smooth, out_ref[at, :])
+                here = tile(p, g)
+                out_ref[here, :] = x_ref[here, :] + jnp.where(polar, smooth, out_ref[here, :])
             return carry
 
         lax.fori_loop(0, 8, rebuild, 0)
@@ -343,10 +374,9 @@
 def on_device(state, damping, cutoff):
     fields, levels, nrow, ncol = state.shape
     bands, blocks = lax.axis_size("lat"), lax.axis_size("lon")
-    lat, lon = lax.axis_index("lat"), lax.axis_index("lon")
     chips = blocks // 2
     vmem, hbm = pl.BlockSpec(memory_space=pltpu.VMEM), pl.BlockSpec(memory_space=pltpu.HBM)
-    params = pltpu.CompilerParams(vmem_limit_bytes=40 * 2**20)
+    limits = pltpu.CompilerParams(vmem_limit_bytes=40 * 2**20)
 
     def call(kernel, name, out, ins, outs, cost, scratch=(), aliases=None):
         return pl.pallas_call(
@@ -355,7 +385,7 @@
             in_specs=ins,
             out_specs=outs,
             scratch_shapes=scratch,
-            compiler_params=params,
+            compiler_params=limits,
             input_output_aliases=aliases or {},
             cost_estimate=pl.CostEstimate(flops=cost, bytes_accessed=2**22, transcendentals=0),
             name=name,
@@ -372,12 +402,6 @@
         parts.reshape(blocks, -1, ncol), "lon", split_axis=0, concat_axis=0, tiled=True
     ).reshape(-1, ncol)
 
-    group = lat * (nrow // ROWS) + lon % 2
-    tables = lax.dynamic_index_in_dim(row_constants(nrow * bands), group, keepdims=False)
-    damp = lax.dynamic_slice(damping, (lon // 2 * 2,), (2,))
-    damp = jnp.broadcast_to(damp[:, None, None], (2, ROWS, ncol))
-    limit = lax.dynamic_slice(cutoff, (group * ROWS,), (ROWS,))
-    limit = jnp.broadcast_to(limit[:, None], (ROWS, ncol))
     twist, forward, inverse = fourier_tables(blocks)
 
     plane = array(10, blocks, ncol)
@@ -398,25 +422,25 @@
     z_other = lax.ppermute(z_mine, ("lat", "lon"), swaps)
     pairs = [[2 * m, 2 * m + 1] for m in range(chips)]
     c_both = lax.all_gather(c_mine, "lon", axis_index_groups=pairs)
-    increments = call(
-        lambda *refs: stencil_kernel(blocks, *refs),
+    increments, params = call(
+        lambda *refs: stencil_kernel(bands, blocks, *refs),
         "stencil",
-        array(*circles.shape),
+        (array(*circles.shape), array(3, ROWS, ncol)),
         [vmem] * 3,
-        vmem,
+        (vmem, vmem),
         2**31,
         [pltpu.VMEM((blocks, 2, ROWS, ncol), jnp.float32)],
-    )(circles, tables, damp)
+    )(circles, damping, cutoff)
     moved = call(
-        lambda *refs: filter_kernel(blocks, *refs),
+        lambda *refs: filter_kernel(bands, blocks, *refs),
         "filter",
         array(*circles.shape),
-        [vmem] * 11,
+        [vmem] * 9,
         vmem,
         2**31,
         [pltpu.VMEM((blocks // 2 + 1, 8 * ROWS, 2 * ncol), jnp.float32)],
         {1: 0},
-    )(circles, increments, z_other, c_both, own, tables, damp, limit, twist, forward, inverse)
+    )(circles, increments, z_other, c_both, own, params, twist, forward, inverse)
 
     home = lax.all_to_all(
         moved.reshape(blocks, -1, ncol), "lon", split_axis=0, concat_axis=0, tiled=True

time: 62.4 us -> 60.9 us (0.976)
  blocking collectives: 22.7 us -> 49.1 us
  waiting for transfers between devices: 16.3 us -> 0.01 us
  starting transfers between devices: 12.4 us -> 2.56 us
  local copies, waits for them, and re-layouts: 2.45 us -> 1.25 us
  Pallas kernels: 8.2 us -> 7.34 us
    all_to_all x0 -> x1, blocking collectives: none -> 26.8 us  [on_device(): lax.all_to_all(parts.reshape(blocks, -1, ncol), 'lon', split_axis=0, conc...]
    all_to_all x1 -> x0, waiting for transfers between devices: 16.2 us -> none  [on_device(): lax.all_to_all(parts.reshape(blocks, -1, ncol), 'lon', split_axis=0, conc...]
    all_to_all x1 -> x0, starting transfers between devices: 10.5 us -> none  [on_device(): lax.all_to_all(parts.reshape(blocks, -1, ncol), 'lon', split_axis=0, conc...]
    pallas_call x1, Pallas kernels: 1.13 us -> 0.16 us  [on_device(): call(spread_kernel, 'spread', array(chips, 2, fields, 2, ROWS, ncol), [hb...]
    squeeze x1 -> x0, local copies, waits for them, and re-layouts: 0.89 us -> none  [on_device(): lax.dynamic_index_in_dim(row_constants(nrow * bands), group, keepdims=False)]
    ppermute x1, starting transfers between devices: 1.92 us -> 2.56 us  [on_device(): z_other = lax.ppermute(z_mine, ('lat', 'lon'), swaps)]
  transfers between devices with their start and end apart: 2 -> 1, of which waited for: 2 -> 0; matrix products, arithmetic and copies ran while one was open for 2% -> 0% of each run, Pallas kernels for 4% -> 4%
where the time goes in v2:
time: 60.9 us; the launch traced here: 60.3 us
  blocking collectives  49.1 us (81%)
  Pallas kernels  7.34 us (12%)
  starting transfers between devices  2.56 us (4%)
  local copies, waits for them, and re-layouts  1.25 us (2%)
    all_to_all x1, blocking collectives, on_device(): lax.all_to_all(parts.reshape(blocks, -1, ncol), 'lon', split_axis=0, conc...  26.8 us
    all_to_all x1, blocking collectives, on_device(): lax.all_to_all(moved.reshape(blocks, -1, ncol), 'lon', split_axis=0, conc...  20.2 us
    pallas_call x1, Pallas kernels, on_device(): call(lambda *refs: filter_kernel(bands, blocks, *refs), 'filter', array(*...  3.34 us
    pallas_call x1, Pallas kernels, on_device(): call(lambda *refs: stencil_kernel(bands, blocks, *refs), 'stencil', (arra...  2.58 us
    ppermute x1, starting transfers between devices, on_device(): z_other = lax.ppermute(z_mine, ('lat', 'lon'), swaps)  2.56 us
    all_gather x1, blocking collectives, on_device(): c_both = lax.all_gather(c_mine, 'lon', axis_index_groups=pairs)  2.04 us
    unnamed x12, local copies, waits for them, and re-layouts  1.25 us
  transfers between devices with their start and end apart: 1, of which 0 were waited for; matrix products, arithmetic and copies ran while one was open for 0% of the time, Pallas kernels for 4%

profile of v2, /device:TPU:1, one launch (start us, length us, event | category | flops | bytes accessed | tf_op | source)
XLA Modules:
  0.0 60.3 jit_solution(4536161583537552467)
XLA Ops:
  0.0 0.0 copy-start
  0.0 1.2 %copy-done = f32[4,32,16,128]{3,2,1,0:T(8,128)S(1)} copy-done((f32[4,32,16,128]{3,2,1,0:T(8,128)S(1)}, f32[4,32,16,128]{3,2,1,0:T(8,128)}, u32[]{:S(2)}) %copy-start) | copy-done | bytes 1048600
  1.2 0.2 spread.1
  1.4 26.8 %all_to_all.10 = f32[32,64,128]{2,1,0:T(8,128)S(1)} all-to-all(f32[32,64,128]{2,1,0:T(8,128)S(1)} %bitcast.11), channel_id=1, replica_groups=mesh['lat'=16,'lon'=32] {'lon'}, dimensions={0} | all-to-all | bytes 2097152 | tf_op jit(solution)/shard_map/all_to_all | solution.py:401
  28.2 0.2 pack.1
  28.5 2.6 %collective-permute-start = (f32[10,32,128]{2,1,0:T(8,128)S(1)}, f32[10,32,128]{2,1,0:T(8,128)S(1)}, u32[]{:S(2)}, u32[]{:S(2)}) collective-permute-start(f32[10,32,128]{2,1,0:T(8,128)S(1)} %get-tuple-element.11), channel_id=1, source_target_pairs={{1,32},{32,1},{3,34},{34,3},{5,36},{36,5},{7,38},{38,7},{9,40},{40... | collective-permute-start | bytes 491528 | tf_op jit(solution)/shard_map/ppermute | solution.py:422
  31.0 0.0 copy-start.1
  31.0 0.0 copy-start.2
  31.1 2.0 %all-gather = f32[20,32,128]{2,1,0:T(8,128)S(1)} all-gather(f32[10,32,128]{2,1,0:T(8,128)S(1)} %get-tuple-element.12), channel_id=2, replica_groups={{0,1},{2,3},{4,5},{6,7},{8,9},{10,11},{12,13},{14,15},{16,17},{18,19},{..., dimensions={0}, use_global_device_ids=true | all-gather | bytes 491520 | tf_op jit(solution)/shard_map/all_gather | solution.py:424
  33.1 0.0 copy-done.1
  33.1 0.0 copy-done.2
  33.1 0.0 copy-start.3
  33.1 0.0 copy-start.4
  33.1 0.0 copy-start.5
  33.1 2.6 %stencil.1 = (f32[2048,128]{1,0:T(8,128)S(1)}, f32[3,8,128]{2,1,0:T(8,128)S(1)}) custom-call(f32[2048,128]{1,0:T(8,128)S(1)} %bitcast.8, f32[32]{0:T(128)S(1)} %copy-done.2, s32[256]{0:T(256)S(1)} %copy-done.1), custom_call_target="tpu_custom_call" | custom-call | flops 2147483648 | bytes 4194304 | tf_op jit(solution)/shard_map/stencil/pallas_call | solution.py:425
  35.7 0.0 collective-permute-done.refs_2_
  35.7 0.0 copy-done.3
  35.7 0.0 copy-done.4
  35.7 0.0 copy-done.5
  35.8 3.3 %filter.1 = f32[2048,128]{1,0:T(8,128)S(1)} custom-call(f32[2048,128]{1,0:T(8,128)S(1)} %bitcast.9, f32[2048,128]{1,0:T(8,128)S(1)} %get-tuple-element.10.refs_1_, f32[10,32,128]{2,1,0:T(8,128)S(1)} %collective-permute-done.refs_2_, f32[2,10,32,128]{3,2,1,0:T(8,128)S(1)} %bitcast.14, ...), custom_call_target="tpu_custom_call", output_to_operand_aliasing={{}: (1, {})} | custom-call | flops 2147483648 | bytes 4194304 | tf_op jit(solution)/shard_map/filter/pallas_call | solution.py:434
  39.1 20.2 %all_to_all.11 = f32[32,64,128]{2,1,0:T(8,128)S(1)} all-to-all(f32[32,64,128]{2,1,0:T(8,128)S(1)} %bitcast.13), channel_id=1, replica_groups=mesh['lat'=16,'lon'=32] {'lon'}, dimensions={0} | all-to-all | bytes 2097152 | tf_op jit(solution)/shard_map/all_to_all | solution.py:445
  59.3 1.0 %collect.1 = f32[4,16,2,2,8,128]{5,4,3,2,1,0:T(8,128)} custom-call(f32[16,2,4,2,8,128]{5,4,3,2,1,0:T(8,128)S(1)} %bitcast.10), custom_call_target="tpu_custom_call" | custom-call | bytes 4194304 | tf_op jit(solution)/shard_map/collect/pallas_call | solution.py:448
Async XLA Ops:
  0.0 1.2 %copy-start = (f32[4,32,16,128]{3,2,1,0:T(8,128)S(1)}, f32[4,32,16,128]{3,2,1,0:T(8,128)}, u32[]{:S(2)}) copy-start(f32[4,32,16,128]{3,2,1,0:T(8,128)} %param.6) | copy-start | bytes 3145732
  28.5 7.3 %collective-permute-start = (f32[10,32,128]{2,1,0:T(8,128)S(1)}, f32[10,32,128]{2,1,0:T(8,128)S(1)}, u32[]{:S(2)}, u32[]{:S(2)}) collective-permute-start(f32[10,32,128]{2,1,0:T(8,128)S(1)} %get-tuple-element.11), channel_id=1, source_target_pairs={{1,32},{32,1},{3,34},{34,3},{5,36},{36,5},{7,38},{38,7},{9,40},{40... | collective-permute-start | bytes 491528 | tf_op jit(solution)/shard_map/ppermute | solution.py:422
  31.0 2.1 %copy-start.1 = (s32[256]{0:T(256)S(1)}, s32[256]{0:T(256)}, u32[]{:S(2)}) copy-start(s32[256]{0:T(256)} %refs_2_.1) | copy-start | bytes 3076
  31.0 2.1 %copy-start.2 = (f32[32]{0:T(128)S(1)}, f32[32]{0:T(128)}, u32[]{:S(2)}) copy-start(f32[32]{0:T(128)} %refs_1_.1) | copy-start | bytes 388
  33.1 2.6 %copy-start.3 = (bf16[2,256,256]{2,1,0:T(8,128)(2,1)S(1)}, bf16[2,256,256]{2,1,0:T(8,128)(2,1)}, u32[]{:S(2)}) copy-start(bf16[2,256,256]{2,1,0:T(8,128)(2,1)} %constant.8.clone.refs_8_) | copy-start | bytes 786436
  33.1 2.6 %copy-start.4 = (bf16[2,256,256]{2,1,0:T(8,128)(2,1)S(1)}, bf16[2,256,256]{2,1,0:T(8,128)(2,1)}, u32[]{:S(2)}) copy-start(bf16[2,256,256]{2,1,0:T(8,128)(2,1)} %constant.7.clone.refs_7_) | copy-start | bytes 786436
  33.1 2.6 %copy-start.5 = (f32[2,17,8,128]{3,2,1,0:T(8,128)S(1)}, f32[2,17,8,128]{3,2,1,0:T(8,128)}, u32[]{:S(2)}) copy-start(f32[2,17,8,128]{3,2,1,0:T(8,128)} %constant.6.clone.refs_6_) | copy-start | bytes 417796

commit v3 on v2

--- a/solution.py
+++ b/solution.py
@@ -227,7 +227,7 @@
             div_ref[p, level] = zonal_diff(x(before, u), x(p, u), x(after, u)) + merid_flux(x(p, v))
         return carry
 
-    lax.fori_loop(0, blocks, divergence, 0, unroll=4)
+    lax.fori_loop(0, blocks, divergence, 0, unroll=blocks)
 
     def increments(p, carry):
         before, after = around(p)
@@ -254,7 +254,7 @@
             )
         return carry
 
-    lax.fori_loop(0, blocks, increments, 0, unroll=2)
+    lax.fori_loop(0, blocks, increments, 0, unroll=blocks)
 
 
 def filter_kernel(
@@ -334,22 +334,29 @@
                 wave_ref[k, at, :LANES], wave_ref[k, at, LANES:] = turned
             return carry
 
-        lax.fori_loop(0, 8, analyse, 0)
+        lax.fori_loop(0, 8, analyse, 0, unroll=8)
 
         def product(values, table_ref):
             high, low = split(values)
             dot = lambda a, b: jnp.dot(a, b, preferred_element_type=jnp.float32)
             return dot(high, table_ref[0]) + dot(low, table_ref[0]) + dot(high, table_ref[1])
 
-        count = (top + 1) * 8 * ROWS
-        spectrum = product(wave_ref[...].reshape(count, 2 * LANES), forward_ref)
-        spectrum = spectrum.reshape(top + 1, 8, ROWS, 2 * LANES)
-        wave = lax.broadcasted_iota(jnp.int32, (top + 1, 1, ROWS, LANES), 0)
-        wave = wave + blocks * lax.broadcasted_iota(jnp.int32, (top + 1, 1, ROWS, LANES), 3)
-        kept = jnp.minimum(wave, nlon - wave) <= limit
-        kept = jnp.concatenate([kept, kept], axis=-1)
-        spectrum = jnp.where(kept, spectrum, 0.0).reshape(count, 2 * LANES)
-        wave_ref[...] = product(spectrum, inverse_ref).reshape(top + 1, 8 * ROWS, 2 * LANES)
+        def middle(start, stop):
+            count = (stop - start) * 8 * ROWS
+            spectrum = product(wave_ref[start:stop].reshape(count, 2 * LANES), forward_ref)
+            spectrum = spectrum.reshape(stop - start, 8, ROWS, 2 * LANES)
+            wave = start + lax.broadcasted_iota(jnp.int32, (stop - start, 1, ROWS, LANES), 0)
+            step = lax.broadcasted_iota(jnp.int32, (stop - start, 1, ROWS, LANES), 3)
+            wave = wave + blocks * step
+            kept = jnp.minimum(wave, nlon - wave) <= limit
+            kept = jnp.concatenate([kept, kept], axis=-1)
+            spectrum = jnp.where(kept, spectrum, 0.0).reshape(count, 2 * LANES)
+            smooth = product(spectrum, inverse_ref)
+            wave_ref[start:stop] = smooth.reshape(stop - start, 8 * ROWS, 2 * LANES)
+
+        edges = [i * (top + 1) // 8 for i in range(9)]
+        for start, stop in zip(edges, edges[1:]):
+            middle(start, stop)
 
         def rebuild(g, carry):
             at = pl.ds(pl.multiple_of(g * ROWS, ROWS), ROWS)
@@ -368,7 +375,7 @@
                 out_ref[here, :] = x_ref[here, :] + jnp.where(polar, smooth, out_ref[here, :])
             return carry
 
-        lax.fori_loop(0, 8, rebuild, 0)
+        lax.fori_loop(0, 8, rebuild, 0, unroll=8)
 
 
 def on_device(state, damping, cutoff):

time: 60.9 us -> 59.5 us (0.977)
  Pallas kernels: 7.34 us -> 4.79 us
  waiting for transfers between devices: 0.01 us -> 1.08 us
    pallas_call x1, Pallas kernels: 2.58 us -> 0.89 us  [on_device(): call(lambda *refs: stencil_kernel(bands, blocks, *refs), 'stencil', (arra...]
    ppermute x1, waiting for transfers between devices: 0.01 us -> 1.08 us  [on_device(): z_other = lax.ppermute(z_mine, ('lat', 'lon'), swaps)]
    pallas_call x1, Pallas kernels: 3.34 us -> 2.48 us  [on_device(): call(lambda *refs: filter_kernel(bands, blocks, *refs), 'filter', array(*...]
  transfers between devices with their start and end apart: 1 -> 1, of which waited for: 0 -> 1; matrix products, arithmetic and copies ran while one was open for 0% -> 0% of each run, Pallas kernels for 4% -> 2%
where the time goes in v3:
time: 59.5 us; the launch traced here: 59.3 us
  blocking collectives  49.5 us (83%)
  Pallas kernels  4.79 us (8%)
  starting transfers between devices  2.56 us (4%)
  local copies, waits for them, and re-layouts  1.25 us (2%)
  waiting for transfers between devices  1.08 us (2%)
    all_to_all x1, blocking collectives, on_device(): lax.all_to_all(parts.reshape(blocks, -1, ncol), 'lon', split_axis=0, conc...  26.8 us
    all_to_all x1, blocking collectives, on_device(): lax.all_to_all(moved.reshape(blocks, -1, ncol), 'lon', split_axis=0, conc...  20.6 us
    ppermute x1, starting transfers between devices, on_device(): z_other = lax.ppermute(z_mine, ('lat', 'lon'), swaps)  2.56 us
    pallas_call x1, Pallas kernels, on_device(): call(lambda *refs: filter_kernel(bands, blocks, *refs), 'filter', array(*...  2.48 us
    all_gather x1, blocking collectives, on_device(): c_both = lax.all_gather(c_mine, 'lon', axis_index_groups=pairs)  2.04 us
    unnamed x12, local copies, waits for them, and re-layouts  1.25 us
  transfers between devices with their start and end apart: 1, of which 1 were waited for; matrix products, arithmetic and copies ran while one was open for 0% of the time, Pallas kernels for 2%

profile of v3, /device:TPU:1, one launch (start us, length us, event | category | flops | bytes accessed | tf_op | source)
XLA Modules:
  0.0 59.3 jit_solution(8621471951607495351)
XLA Ops:
  0.0 0.0 copy-start
  0.0 1.2 %copy-done = f32[4,32,16,128]{3,2,1,0:T(8,128)S(1)} copy-done((f32[4,32,16,128]{3,2,1,0:T(8,128)S(1)}, f32[4,32,16,128]{3,2,1,0:T(8,128)}, u32[]{:S(2)}) %copy-start) | copy-done | bytes 1048600
  1.2 0.2 spread.1
  1.4 26.8 %all_to_all.10 = f32[32,64,128]{2,1,0:T(8,128)S(1)} all-to-all(f32[32,64,128]{2,1,0:T(8,128)S(1)} %bitcast.11), channel_id=1, replica_groups=mesh['lat'=16,'lon'=32] {'lon'}, dimensions={0} | all-to-all | bytes 2097152 | tf_op jit(solution)/shard_map/all_to_all | solution.py:408
  28.2 0.2 pack.1
  28.5 2.6 %collective-permute-start = (f32[10,32,128]{2,1,0:T(8,128)S(1)}, f32[10,32,128]{2,1,0:T(8,128)S(1)}, u32[]{:S(2)}, u32[]{:S(2)}) collective-permute-start(f32[10,32,128]{2,1,0:T(8,128)S(1)} %get-tuple-element.11), channel_id=1, source_target_pairs={{1,32},{32,1},{3,34},{34,3},{5,36},{36,5},{7,38},{38,7},{9,40},{40... | collective-permute-start | bytes 491528 | tf_op jit(solution)/shard_map/ppermute | solution.py:429
  31.0 0.0 copy-start.1
  31.0 0.0 copy-start.2
  31.1 2.0 %all-gather = f32[20,32,128]{2,1,0:T(8,128)S(1)} all-gather(f32[10,32,128]{2,1,0:T(8,128)S(1)} %get-tuple-element.12), channel_id=2, replica_groups={{0,1},{2,3},{4,5},{6,7},{8,9},{10,11},{12,13},{14,15},{16,17},{18,19},{..., dimensions={0}, use_global_device_ids=true | all-gather | bytes 491520 | tf_op jit(solution)/shard_map/all_gather | solution.py:431
  33.1 0.0 copy-done.1
  33.1 0.0 copy-done.2
  33.1 0.0 copy-start.3
  33.1 0.0 copy-start.4
  33.1 0.0 copy-start.5
  33.1 0.9 %stencil.1 = (f32[2048,128]{1,0:T(8,128)S(1)}, f32[3,8,128]{2,1,0:T(8,128)S(1)}) custom-call(f32[2048,128]{1,0:T(8,128)S(1)} %bitcast.8, f32[32]{0:T(128)S(1)} %copy-done.2, s32[256]{0:T(256)S(1)} %copy-done.1), custom_call_target="tpu_custom_call" | custom-call | flops 2147483648 | bytes 4194304 | tf_op jit(solution)/shard_map/stencil/pallas_call | solution.py:432
  34.0 1.1 %collective-permute-done.refs_2_ = f32[10,32,128]{2,1,0:T(8,128)S(1)} collective-permute-done((f32[10,32,128]{2,1,0:T(8,128)S(1)}, f32[10,32,128]{2,1,0:T(8,128)S(1)}, u32[]{:S(2)}, u32[]{:S(2)}) %collective-permute-start) | collective-permute-done | bytes 163872 | tf_op jit(solution)/shard_map/ppermute | solution.py:429
  35.1 0.0 copy-done.3
  35.1 0.0 copy-done.4
  35.1 0.0 copy-done.5
  35.1 2.5 %filter.1 = f32[2048,128]{1,0:T(8,128)S(1)} custom-call(f32[2048,128]{1,0:T(8,128)S(1)} %bitcast.9, f32[2048,128]{1,0:T(8,128)S(1)} %get-tuple-element.10.refs_1_, f32[10,32,128]{2,1,0:T(8,128)S(1)} %collective-permute-done.refs_2_, f32[2,10,32,128]{3,2,1,0:T(8,128)S(1)} %bitcast.14, ...), custom_call_target="tpu_custom_call", output_to_operand_aliasing={{}: (1, {})} | custom-call | flops 2147483648 | bytes 4194304 | tf_op jit(solution)/shard_map/filter/pallas_call | solution.py:441
  37.6 20.6 %all_to_all.11 = f32[32,64,128]{2,1,0:T(8,128)S(1)} all-to-all(f32[32,64,128]{2,1,0:T(8,128)S(1)} %bitcast.13), channel_id=1, replica_groups=mesh['lat'=16,'lon'=32] {'lon'}, dimensions={0} | all-to-all | bytes 2097152 | tf_op jit(solution)/shard_map/all_to_all | solution.py:452
  58.2 1.0 %collect.1 = f32[4,16,2,2,8,128]{5,4,3,2,1,0:T(8,128)} custom-call(f32[16,2,4,2,8,128]{5,4,3,2,1,0:T(8,128)S(1)} %bitcast.10), custom_call_target="tpu_custom_call" | custom-call | bytes 4194304 | tf_op jit(solution)/shard_map/collect/pallas_call | solution.py:455
Async XLA Ops:
  0.0 1.2 %copy-start = (f32[4,32,16,128]{3,2,1,0:T(8,128)S(1)}, f32[4,32,16,128]{3,2,1,0:T(8,128)}, u32[]{:S(2)}) copy-start(f32[4,32,16,128]{3,2,1,0:T(8,128)} %param.6) | copy-start | bytes 3145732
  28.5 6.6 %collective-permute-start = (f32[10,32,128]{2,1,0:T(8,128)S(1)}, f32[10,32,128]{2,1,0:T(8,128)S(1)}, u32[]{:S(2)}, u32[]{:S(2)}) collective-permute-start(f32[10,32,128]{2,1,0:T(8,128)S(1)} %get-tuple-element.11), channel_id=1, source_target_pairs={{1,32},{32,1},{3,34},{34,3},{5,36},{36,5},{7,38},{38,7},{9,40},{40... | collective-permute-start | bytes 491528 | tf_op jit(solution)/shard_map/ppermute | solution.py:429
  31.0 2.1 %copy-start.1 = (s32[256]{0:T(256)S(1)}, s32[256]{0:T(256)}, u32[]{:S(2)}) copy-start(s32[256]{0:T(256)} %refs_2_.1) | copy-start | bytes 3076
  31.0 2.1 %copy-start.2 = (f32[32]{0:T(128)S(1)}, f32[32]{0:T(128)}, u32[]{:S(2)}) copy-start(f32[32]{0:T(128)} %refs_1_.1) | copy-start | bytes 388
  33.1 2.0 %copy-start.3 = (bf16[2,256,256]{2,1,0:T(8,128)(2,1)S(1)}, bf16[2,256,256]{2,1,0:T(8,128)(2,1)}, u32[]{:S(2)}) copy-start(bf16[2,256,256]{2,1,0:T(8,128)(2,1)} %constant.8.clone.refs_8_) | copy-start | bytes 786436
  33.1 2.0 %copy-start.4 = (bf16[2,256,256]{2,1,0:T(8,128)(2,1)S(1)}, bf16[2,256,256]{2,1,0:T(8,128)(2,1)}, u32[]{:S(2)}) copy-start(bf16[2,256,256]{2,1,0:T(8,128)(2,1)} %constant.7.clone.refs_7_) | copy-start | bytes 786436
  33.1 2.0 %copy-start.5 = (f32[2,17,8,128]{3,2,1,0:T(8,128)S(1)}, f32[2,17,8,128]{3,2,1,0:T(8,128)}, u32[]{:S(2)}) copy-start(f32[2,17,8,128]{3,2,1,0:T(8,128)} %constant.6.clone.refs_6_) | copy-start | bytes 417796

commit v4 on v2

--- a/solution.py
+++ b/solution.py
@@ -47,7 +47,7 @@
         row = self.first + (ROWS if side else -1)
         inside = ((row >= 0) & (row < self.nlat)).astype(jnp.float32)
         half = 0.5 / at * inside
-        return half, above * half, below * half, inside
+        return (-below if side else above) * half, inside
 
 
 def split(values):
@@ -150,17 +150,31 @@
         copy.wait()
 
 
-def pack_kernel(blocks, x_ref, z_ref, c_ref, own_ref):
-    core = lax.axis_index("lon") % 2
+def shifted_diff(here):
+    blocks = here.shape[0]
+    lane = lax.broadcasted_iota(jnp.int32, here.shape, 1)
+    after = jnp.where(lane == 0, pltpu.roll(here, blocks - 1, axis=0), here)
+    before = jnp.where(lane == LANES - 1, pltpu.roll(here, 1, axis=0), here)
+    return pltpu.roll(after, LANES - 1, axis=1) - pltpu.roll(before, 1, axis=1)
+
+
+def pack_kernel(bands, blocks, x_ref, z_ref, c_ref, own_ref):
+    rows = Rows(bands)
 
     def plane(field, level, row):
         return x_ref[pl.ds((field * 2 + level) * ROWS + row, blocks, stride=8 * ROWS), :]
 
-    for out, end in ((z_ref, core), (c_ref, 1 - core)):
+    for out, end in ((z_ref, rows.core), (c_ref, 1 - rows.core)):
         edge, inner = end * (ROWS - 1), 1 + end * (ROWS - 3)
-        for k, (field, row) in enumerate(((0, edge), (1, edge), (3, edge), (2, edge), (2, inner))):
-            for level in range(2):
-                out[k * 2 + level] = plane(field, level, row)
+        half, weight = (
+            jnp.where(end == 1, v[ROWS - 1 :], w[:1])
+            for v, w in ((rows.half, rows.half), (-rows.down, rows.up))
+        )
+        for level in range(2):
+            for k, field in enumerate((0, 2, 3)):
+                out[k * 2 + level] = plane(field, level, edge)
+            zonal, far = plane(1, level, edge), plane(2, level, inner)
+            out[6 + level] = shifted_diff(zonal) * half + weight * far
     for side in range(2):
         for level in range(2):
             own_ref[side * 2 + level] = plane(2, level, side * (ROWS - 1))
@@ -182,10 +196,11 @@
 
 
 def tile(p, g):
-    return pl.ds(pl.multiple_of((p * 8 + g) * ROWS, ROWS), ROWS)
-
-
-def stencil_kernel(bands, blocks, x_ref, damp_ref, cutoff_ref, inc_ref, param_ref, div_ref):
+    start = (p * 8 + g) * ROWS
+    return pl.ds(start if isinstance(start, int) else pl.multiple_of(start, ROWS), ROWS)
+
+
+def stencil_kernel(bands, blocks, x_ref, damp_ref, cutoff_ref, inc_ref, param_ref, mix_ref):
     rows = Rows(bands)
     parameters(rows, damp_ref, cutoff_ref, param_ref)
     row = lax.broadcasted_iota(jnp.int32, (ROWS, LANES), 0)
@@ -208,53 +223,51 @@
     def south(here):
         return pltpu.roll(here, 1, axis=0)
 
-    def merid_flux(here):
-        return up * north(here) - down * south(here)
-
-    def merid_diff(here):
-        return half_up * north(here) - half_down * south(here)
-
     def x(p, g):
         return x_ref[tile(p, g), :]
 
     def around(p):
         return lax.rem(p + blocks - 1, blocks), lax.rem(p + 1, blocks)
 
-    def divergence(p, carry):
+    damping_north = [south(v) for v in damping]
+    damping_south = [north(v) for v in damping]
+
+    def first_pass(p, carry):
         before, after = around(p)
         for level in range(2):
-            u, v = 2 + level, 4 + level
-            div_ref[p, level] = zonal_diff(x(before, u), x(p, u), x(after, u)) + merid_flux(x(p, v))
+            h, u, v = level, 2 + level, 4 + level
+            thick, zonal = COURANT * x(p, h), x(p, u)
+            div = zonal_diff(x(before, u), zonal, x(after, u))
+            div = div + up * north(x(p, v)) - down * south(x(p, v))
+            mix_ref[p, level] = damping[level] * div - thick
+            rise = half_up * north(damping_north[level] * div - thick)
+            rise = rise - half_down * south(damping_south[level] * div - thick)
+            inc_ref[tile(p, v), :] = rise - COURANT * (rows.coriolis * zonal)
         return carry
 
-    lax.fori_loop(0, blocks, divergence, 0, unroll=4)
-
-    def increments(p, carry):
+    lax.fori_loop(0, blocks, first_pass, 0, unroll=blocks)
+
+    def second_pass(p, carry):
         before, after = around(p)
         for level in range(2):
             h, u, v, t = level, 2 + level, 4 + level, 6 + level
-            damp = damping[level]
-            thick, zonal, merid, potential = x(p, h), x(p, u), x(p, v), x(p, t)
-            thick_b, thick_a = x(before, h), x(after, h)
-            carried = 1.0 + thick
-            flux_b, flux_a = (1.0 + thick_b) * x(before, u), (1.0 + thick_a) * x(after, u)
+            zonal, merid, potential = x(p, u), x(p, v), x(p, t)
+            carried = 1.0 + x(p, h)
+            flux_b, flux_a = (1.0 + x(before, h)) * x(before, u), (1.0 + x(after, h)) * x(after, u)
+            flow = carried * merid
             inc_ref[tile(p, h), :] = -COURANT * (
-                zonal_diff(flux_b, carried * zonal, flux_a) + merid_flux(carried * merid)
+                zonal_diff(flux_b, carried * zonal, flux_a) + up * north(flow) - down * south(flow)
             )
-            div = div_ref[p, level]
-            inc_ref[tile(p, u), :] = COURANT * (
-                rows.coriolis * merid - zonal_diff(thick_b, thick, thick_a)
-            ) + damp * zonal_diff(div_ref[before, level], div, div_ref[after, level])
-            inc_ref[tile(p, v), :] = damp * merid_diff(div) - COURANT * (
-                rows.coriolis * zonal + merid_diff(thick)
+            inc_ref[tile(p, u), :] = COURANT * (rows.coriolis * merid) + zonal_diff(
+                mix_ref[before, level], mix_ref[p, level], mix_ref[after, level]
             )
+            rise = half_up * north(potential) - half_down * south(potential)
             inc_ref[tile(p, t), :] = -COURANT * (
-                zonal * zonal_diff(x(before, t), potential, x(after, t))
-                + merid * merid_diff(potential)
+                zonal * zonal_diff(x(before, t), potential, x(after, t)) + merid * rise
             )
         return carry
 
-    lax.fori_loop(0, blocks, increments, 0, unroll=2)
+    lax.fori_loop(0, blocks, second_pass, 0, unroll=blocks)
 
 
 def filter_kernel(
@@ -270,25 +283,14 @@
     forward_ref,
     inverse_ref,
     out_ref,
+    more_ref,
     wave_ref,
 ):
-    del inc_ref
     rows = Rows(bands)
     damping = [rows.square * param_ref[i] for i in range(2)]
-    lane = lax.broadcasted_iota(jnp.int32, (blocks, LANES), 1)
-
-    def shifted_diff(v):
-        after = jnp.where(lane == 0, pltpu.roll(v, blocks - 1, axis=0), v)
-        before = jnp.where(lane == LANES - 1, pltpu.roll(v, 1, axis=0), v)
-        return pltpu.roll(after, LANES - 1, axis=1) - pltpu.roll(before, 1, axis=1)
-
-    def add(group, row, value):
-        at = pl.ds(group * ROWS + row, blocks, stride=8 * ROWS)
-        out_ref[at, :] = out_ref[at, :] + value
-
     for side in range(2):
         edge, inner = side * (ROWS - 1), 1 + side * (ROWS - 3)
-        half, up, down, inside = rows.beside(side)
+        across, inside = rows.beside(side)
         weight = rows.up[edge : edge + 1] if side else -rows.down[edge : edge + 1]
         step = 0.5 if side else -0.5
         for level in range(2):
@@ -299,76 +301,101 @@
                 other = c_ref[1 - rows.core, k * 2 + level]
                 return jnp.where(rows.core == side, z_ref[k * 2 + level], other) * inside
 
-            thick, zonal, potential, near, far = (beyond(k) for k in range(5))
+            thick, near, potential, div = (beyond(k) for k in range(4))
             own = own_ref[side * 2 + level]
-            above, below = (far, own) if side else (own, far)
-            div = shifted_diff(zonal) * half + up * above - down * below
-            more = weight * near
-            add(level, edge, -COURANT * weight * ((1.0 + thick) * near))
-            add(2 + level, edge, damp_edge * rows.half[edge : edge + 1] * shifted_diff(more))
-            add(4 + level, edge, step * (damp_edge * div - COURANT * thick))
-            add(4 + level, inner, step * damp_inner * more)
-            add(6 + level, edge, -COURANT * step * (own * potential))
-
-    polar = rows.polar
+            div = div + across * own
+            extra = weight * near
+            more_ref[side, level] = -COURANT * weight * ((1.0 + thick) * near)
+            more_ref[side, 2 + level] = damp_edge * rows.half[edge : edge + 1] * shifted_diff(extra)
+            more_ref[side, 4 + level] = step * (damp_edge * div - COURANT * thick)
+            more_ref[side, 6 + level] = -COURANT * step * (own * potential)
+            more_ref[side, 8 + level] = step * damp_inner * extra
+
+    row = lax.broadcasted_iota(jnp.int32, (ROWS, LANES), 0)
+
+    def increment(p, g):
+        def more(side, k):
+            return more_ref[side, k, p : p + 1, :]
+
+        total = jnp.where(row == 0, more(0, g), jnp.where(row == ROWS - 1, more(1, g), 0.0))
+        if g // 2 == 2:
+            total = jnp.where(row == 1, more(0, g + 4), total)
+            total = jnp.where(row == ROWS - 2, more(1, g + 4), total)
+        return inc_ref[tile(p, g), :] + total
+
     limit = param_ref[2].astype(jnp.int32)
     any_polar = (rows.first < rows.nlat // 4) | (rows.first + ROWS > rows.nlat - rows.nlat // 4)
+    whole = rows.nlat // 4 % ROWS == 0
     top = blocks // 2
     nlon = blocks * LANES
 
     @pl.when(jnp.logical_not(any_polar))
     def _():
-        out_ref[...] = x_ref[...] + out_ref[...]
+        for g in range(8):
+            for p in range(blocks):
+                out_ref[tile(p, g), :] = x_ref[tile(p, g), :] + increment(p, g)
 
     @pl.when(any_polar)
     def _():
-        def analyse(g, carry):
-            waves = real_fft([out_ref[tile(p, g), :] for p in range(blocks)])
-            at = pl.ds(pl.multiple_of(g * ROWS, ROWS), ROWS)
-            for k, (re, im) in enumerate(waves):
-                c, s = twist_ref[0, k], twist_ref[1, k]
-                if im is None:
-                    turned = (re, jnp.zeros_like(re)) if k == 0 else (re * c, -(re * s))
-                else:
-                    turned = (re * c + im * s, im * c - re * s)
-                wave_ref[k, at, :LANES], wave_ref[k, at, LANES:] = turned
-            return carry
-
-        lax.fori_loop(0, 8, analyse, 0)
+        width = 2
+
+        def analyse(part):
+            for i in range(width):
+                waves = real_fft([increment(p, part * width + i) for p in range(blocks)])
+                at = slice(i * ROWS, (i + 1) * ROWS)
+                for k, (re, im) in enumerate(waves):
+                    c, s = twist_ref[0, k], twist_ref[1, k]
+                    if im is None:
+                        turned = (re, jnp.zeros_like(re)) if k == 0 else (re * c, -(re * s))
+                    else:
+                        turned = (re * c + im * s, im * c - re * s)
+                    wave_ref[part, k, at, :LANES], wave_ref[part, k, at, LANES:] = turned
 
         def product(values, table_ref):
             high, low = split(values)
             dot = lambda a, b: jnp.dot(a, b, preferred_element_type=jnp.float32)
-            return dot(high, table_ref[0]) + dot(low, table_ref[0]) + dot(high, table_ref[1])
-
-        count = (top + 1) * 8 * ROWS
-        spectrum = product(wave_ref[...].reshape(count, 2 * LANES), forward_ref)
-        spectrum = spectrum.reshape(top + 1, 8, ROWS, 2 * LANES)
+            return dot(low, table_ref[0]) + dot(high, table_ref[0]) + dot(high, table_ref[1])
+
         wave = lax.broadcasted_iota(jnp.int32, (top + 1, 1, ROWS, LANES), 0)
         wave = wave + blocks * lax.broadcasted_iota(jnp.int32, (top + 1, 1, ROWS, LANES), 3)
         kept = jnp.minimum(wave, nlon - wave) <= limit
         kept = jnp.concatenate([kept, kept], axis=-1)
-        spectrum = jnp.where(kept, spectrum, 0.0).reshape(count, 2 * LANES)
-        wave_ref[...] = product(spectrum, inverse_ref).reshape(top + 1, 8 * ROWS, 2 * LANES)
-
-        def rebuild(g, carry):
-            at = pl.ds(pl.multiple_of(g * ROWS, ROWS), ROWS)
-            waves = []
-            for k in range(top + 1):
-                re, im = wave_ref[k, at, :LANES], wave_ref[k, at, LANES:]
-                c, s = twist_ref[0, k], twist_ref[1, k]
-                if k == 0:
-                    waves.append((re, None))
-                elif k == top:
-                    waves.append((re * c - im * s, None))
-                else:
-                    waves.append((re * c - im * s, im * c + re * s))
-            for p, smooth in enumerate(real_ifft(waves)):
-                here = tile(p, g)
-                out_ref[here, :] = x_ref[here, :] + jnp.where(polar, smooth, out_ref[here, :])
-            return carry
-
-        lax.fori_loop(0, 8, rebuild, 0)
+
+        def middle(part):
+            count = (top + 1) * width * ROWS
+            spectrum = product(wave_ref[part].reshape(count, 2 * LANES), forward_ref)
+            spectrum = spectrum.reshape(top + 1, width, ROWS, 2 * LANES)
+            spectrum = jnp.where(kept, spectrum, 0.0).reshape(count, 2 * LANES)
+            smooth = product(spectrum, inverse_ref)
+            wave_ref[part] = smooth.reshape(top + 1, width * ROWS, 2 * LANES)
+
+        def rebuild(part):
+            for i in range(width):
+                g = part * width + i
+                at = slice(i * ROWS, (i + 1) * ROWS)
+                waves = []
+                for k in range(top + 1):
+                    re, im = wave_ref[part, k, at, :LANES], wave_ref[part, k, at, LANES:]
+                    c, s = twist_ref[0, k], twist_ref[1, k]
+                    if k == 0:
+                        waves.append((re, None))
+                    elif k == top:
+                        waves.append((re * c - im * s, None))
+                    else:
+                        waves.append((re * c - im * s, im * c + re * s))
+                for p, smooth in enumerate(real_ifft(waves)):
+                    if not whole:
+                        smooth = jnp.where(rows.polar, smooth, increment(p, g))
+                    out_ref[tile(p, g), :] = x_ref[tile(p, g), :] + smooth
+
+        parts = 8 // width
+        for i in range(parts + 2):
+            if i < parts:
+                analyse(i)
+            if 1 <= i <= parts:
+                middle(i - 1)
+            if i >= 2:
+                rebuild(i - 2)
 
 
 def on_device(state, damping, cutoff):
@@ -378,7 +405,7 @@
     vmem, hbm = pl.BlockSpec(memory_space=pltpu.VMEM), pl.BlockSpec(memory_space=pltpu.HBM)
     limits = pltpu.CompilerParams(vmem_limit_bytes=40 * 2**20)
 
-    def call(kernel, name, out, ins, outs, cost, scratch=(), aliases=None):
+    def call(kernel, name, out, ins, outs, cost, scratch=()):
         return pl.pallas_call(
             kernel,
             out_shape=out,
@@ -386,7 +413,6 @@
             out_specs=outs,
             scratch_shapes=scratch,
             compiler_params=limits,
-            input_output_aliases=aliases or {},
             cost_estimate=pl.CostEstimate(flops=cost, bytes_accessed=2**22, transcendentals=0),
             name=name,
         )
@@ -404,9 +430,9 @@
 
     twist, forward, inverse = fourier_tables(blocks)
 
-    plane = array(10, blocks, ncol)
+    plane = array(8, blocks, ncol)
     z_mine, c_mine, own = call(
-        lambda *refs: pack_kernel(blocks, *refs),
+        lambda *refs: pack_kernel(bands, blocks, *refs),
         "pack",
         (plane, plane, array(4, blocks, ncol)),
         [vmem],
@@ -428,7 +454,7 @@
         (array(*circles.shape), array(3, ROWS, ncol)),
         [vmem] * 3,
         (vmem, vmem),
-        2**31,
+        2**28,
         [pltpu.VMEM((blocks, 2, ROWS, ncol), jnp.float32)],
     )(circles, damping, cutoff)
     moved = call(
@@ -438,8 +464,10 @@
         [vmem] * 9,
         vmem,
         2**31,
-        [pltpu.VMEM((blocks // 2 + 1, 8 * ROWS, 2 * ncol), jnp.float32)],
-        {1: 0},
+        [
+            pltpu.VMEM((2, 10, blocks, ncol), jnp.float32),
+            pltpu.VMEM((4, blocks // 2 + 1, 2 * ROWS, 2 * ncol), jnp.float32),
+        ],
     )(circles, increments, z_other, c_both, own, params, twist, forward, inverse)
 
     home = lax.all_to_all(

time: 60.9 us -> 58.9 us (0.967)
  Pallas kernels: 7.34 us -> 4.39 us
  waiting for transfers between devices: 0.01 us -> 0.72 us
    pallas_call x1, Pallas kernels: 2.58 us -> 0.81 us  [on_device(): call(lambda *refs: stencil_kernel(bands, blocks, *refs), 'stencil', (arra...]
    pallas_call x1, Pallas kernels: 3.34 us -> 2.14 us  [on_device(): call(lambda *refs: filter_kernel(bands, blocks, *refs), 'filter', array(*...]
    ppermute x1, waiting for transfers between devices: 0.01 us -> 0.72 us  [on_device(): z_other = lax.ppermute(z_mine, ('lat', 'lon'), swaps)]
  transfers between devices with their start and end apart: 1 -> 1, of which waited for: 0 -> 1; matrix products, arithmetic and copies ran while one was open for 0% -> 0% of each run, Pallas kernels for 4% -> 1%
where the time goes in v4:
time: 58.9 us; the launch traced here: 58.6 us
  blocking collectives  49.6 us (84%)
  Pallas kernels  4.39 us (7%)
  starting transfers between devices  2.56 us (4%)
  local copies, waits for them, and re-layouts  1.26 us (2%)
  waiting for transfers between devices  0.72 us (1%)
    all_to_all x1, blocking collectives, on_device(): lax.all_to_all(parts.reshape(blocks, -1, ncol), 'lon', split_axis=0, conc...  26.8 us
    all_to_all x1, blocking collectives, on_device(): lax.all_to_all(moved.reshape(blocks, -1, ncol), 'lon', split_axis=0, conc...  20.6 us
    ppermute x1, starting transfers between devices, on_device(): z_other = lax.ppermute(z_mine, ('lat', 'lon'), swaps)  2.56 us
    pallas_call x1, Pallas kernels, on_device(): call(lambda *refs: filter_kernel(bands, blocks, *refs), 'filter', array(*...  2.14 us
    all_gather x1, blocking collectives, on_device(): c_both = lax.all_gather(c_mine, 'lon', axis_index_groups=pairs)  2.13 us
    unnamed x12, local copies, waits for them, and re-layouts  1.26 us
  transfers between devices with their start and end apart: 1, of which 1 were waited for; matrix products, arithmetic and copies ran while one was open for 0% of the time, Pallas kernels for 1%

profile of v4, /device:TPU:1, one launch (start us, length us, event | category | flops | bytes accessed | tf_op | source)
XLA Modules:
  0.0 58.6 jit_solution(14710563579379451037)
XLA Ops:
  0.0 0.0 copy-start
  0.0 1.2 %copy-done = f32[4,32,16,128]{3,2,1,0:T(8,128)S(1)} copy-done((f32[4,32,16,128]{3,2,1,0:T(8,128)S(1)}, f32[4,32,16,128]{3,2,1,0:T(8,128)}, u32[]{:S(2)}) %copy-start) | copy-done | bytes 1048600
  1.2 0.2 spread.1
  1.4 26.8 %all_to_all.10 = f32[32,64,128]{2,1,0:T(8,128)S(1)} all-to-all(f32[32,64,128]{2,1,0:T(8,128)S(1)} %bitcast.11), channel_id=1, replica_groups=mesh['lat'=16,'lon'=32] {'lon'}, dimensions={0} | all-to-all | bytes 2097152 | tf_op jit(solution)/shard_map/all_to_all | solution.py:427
  28.2 0.3 pack.1
  28.5 0.0 copy-start.1
  28.5 0.0 copy-start.2
  28.5 2.6 %collective-permute-start = (f32[8,32,128]{2,1,0:T(8,128)S(1)}, f32[8,32,128]{2,1,0:T(8,128)S(1)}, u32[]{:S(2)}, u32[]{:S(2)}) collective-permute-start(f32[8,32,128]{2,1,0:T(8,128)S(1)} %get-tuple-element.11), channel_id=1, source_target_pairs={{1,32},{32,1},{3,34},{34,3},{5,36},{36,5},{7,38},{38,7},{9,40},{40... | collective-permute-start | bytes 393224 | tf_op jit(solution)/shard_map/ppermute | solution.py:448
  31.1 0.0 copy-done.1
  31.1 0.0 copy-done.2
  31.1 0.0 copy-start.4
  31.1 0.8 %stencil.1 = (f32[2048,128]{1,0:T(8,128)S(1)}, f32[3,8,128]{2,1,0:T(8,128)S(1)}) custom-call(f32[2048,128]{1,0:T(8,128)S(1)} %bitcast.8, f32[32]{0:T(128)S(1)} %copy-done.2, s32[256]{0:T(256)S(1)} %copy-done.1), custom_call_target="tpu_custom_call" | custom-call | flops 268435456 | bytes 4194304 | tf_op jit(solution)/shard_map/stencil/pallas_call | solution.py:451
  31.9 0.0 copy-start.3
  31.9 0.0 copy-start.5
  32.0 2.1 %all-gather = f32[16,32,128]{2,1,0:T(8,128)S(1)} all-gather(f32[8,32,128]{2,1,0:T(8,128)S(1)} %get-tuple-element.12), channel_id=2, replica_groups={{0,1},{2,3},{4,5},{6,7},{8,9},{10,11},{12,13},{14,15},{16,17},{18,19},{..., dimensions={0}, use_global_device_ids=true | all-gather | bytes 393216 | tf_op jit(solution)/shard_map/all_gather | solution.py:450
  34.1 0.7 %collective-permute-done.refs_2_ = f32[8,32,128]{2,1,0:T(8,128)S(1)} collective-permute-done((f32[8,32,128]{2,1,0:T(8,128)S(1)}, f32[8,32,128]{2,1,0:T(8,128)S(1)}, u32[]{:S(2)}, u32[]{:S(2)}) %collective-permute-start) | collective-permute-done | bytes 131104 | tf_op jit(solution)/shard_map/ppermute | solution.py:448
  34.8 0.0 copy-done.4
  34.8 0.0 copy-done.3
  34.8 0.0 copy-done.5
  34.8 2.1 %filter.1 = f32[2048,128]{1,0:T(8,128)S(1)} custom-call(f32[2048,128]{1,0:T(8,128)S(1)} %bitcast.9, f32[2048,128]{1,0:T(8,128)S(1)} %get-tuple-element.10.refs_1_, f32[8,32,128]{2,1,0:T(8,128)S(1)} %collective-permute-done.refs_2_, f32[2,8,32,128]{3,2,1,0:T(8,128)S(1)} %bitcast.14, f32[4,32,128]{2,1,0:T(8,128)S(1)} %get-tuple-element.13.refs_4_, ...), custom_call_target="tpu_custom_call" | custom-call | flops 2147483648 | bytes 4194304 | tf_op jit(solution)/shard_map/filter/pallas_call | solution.py:460
  37.0 20.6 %all_to_all.11 = f32[32,64,128]{2,1,0:T(8,128)S(1)} all-to-all(f32[32,64,128]{2,1,0:T(8,128)S(1)} %bitcast.13), channel_id=1, replica_groups=mesh['lat'=16,'lon'=32] {'lon'}, dimensions={0} | all-to-all | bytes 2097152 | tf_op jit(solution)/shard_map/all_to_all | solution.py:473
  57.6 1.0 %collect.1 = f32[4,16,2,2,8,128]{5,4,3,2,1,0:T(8,128)} custom-call(f32[16,2,4,2,8,128]{5,4,3,2,1,0:T(8,128)S(1)} %bitcast.10), custom_call_target="tpu_custom_call" | custom-call | bytes 4194304 | tf_op jit(solution)/shard_map/collect/pallas_call | solution.py:476
Async XLA Ops:
  0.0 1.2 %copy-start = (f32[4,32,16,128]{3,2,1,0:T(8,128)S(1)}, f32[4,32,16,128]{3,2,1,0:T(8,128)}, u32[]{:S(2)}) copy-start(f32[4,32,16,128]{3,2,1,0:T(8,128)} %param.6) | copy-start | bytes 3145732
  28.5 2.6 %copy-start.1 = (s32[256]{0:T(256)S(1)}, s32[256]{0:T(256)}, u32[]{:S(2)}) copy-start(s32[256]{0:T(256)} %refs_2_.1) | copy-start | bytes 3076
  28.5 2.6 %copy-start.2 = (f32[32]{0:T(128)S(1)}, f32[32]{0:T(128)}, u32[]{:S(2)}) copy-start(f32[32]{0:T(128)} %refs_1_.1) | copy-start | bytes 388
  28.5 6.3 %collective-permute-start = (f32[8,32,128]{2,1,0:T(8,128)S(1)}, f32[8,32,128]{2,1,0:T(8,128)S(1)}, u32[]{:S(2)}, u32[]{:S(2)}) collective-permute-start(f32[8,32,128]{2,1,0:T(8,128)S(1)} %get-tuple-element.11), channel_id=1, source_target_pairs={{1,32},{32,1},{3,34},{34,3},{5,36},{36,5},{7,38},{38,7},{9,40},{40... | collective-permute-start | bytes 393224 | tf_op jit(solution)/shard_map/ppermute | solution.py:448
  31.1 3.7 %copy-start.4 = (bf16[2,256,256]{2,1,0:T(8,128)(2,1)S(1)}, bf16[2,256,256]{2,1,0:T(8,128)(2,1)}, u32[]{:S(2)}) copy-start(bf16[2,256,256]{2,1,0:T(8,128)(2,1)} %constant.7.clone.refs_7_) | copy-start | bytes 786436
  31.9 2.9 %copy-start.3 = (bf16[2,256,256]{2,1,0:T(8,128)(2,1)S(1)}, bf16[2,256,256]{2,1,0:T(8,128)(2,1)}, u32[]{:S(2)}) copy-start(bf16[2,256,256]{2,1,0:T(8,128)(2,1)} %constant.8.clone.refs_8_) | copy-start | bytes 786436
  31.9 2.9 %copy-start.5 = (f32[2,17,8,128]{3,2,1,0:T(8,128)S(1)}, f32[2,17,8,128]{3,2,1,0:T(8,128)}, u32[]{:S(2)}) copy-start(f32[2,17,8,128]{3,2,1,0:T(8,128)} %constant.6.clone.refs_6_) | copy-start | bytes 417796

commit v5 on v4

--- a/solution.py
+++ b/solution.py
@@ -63,8 +63,9 @@
     cos, sin = np.cos(phase), np.sin(phase)
     forward = np.block([[cos, -sin], [sin, cos]])
     inverse = np.block([[cos, sin], [-sin, cos]]) / nlon
-    turn = 2.0 * np.pi * np.arange(blocks // 2 + 1)[:, None] * at[None, :] / nlon
-    twist = np.stack([np.cos(turn), np.sin(turn)]).astype(np.float32)
+    angle = 2.0 * np.pi * np.arange(blocks // 2 + 1)[:, None] * at[None, :] / nlon
+    twice = np.where(np.arange(blocks // 2 + 1) % (blocks // 2) == 0, 1.0, math.sqrt(2.0))[:, None]
+    twist = np.stack([twice * np.cos(angle), twice * np.sin(angle)]).astype(np.float32)
     twist = np.broadcast_to(twist[:, :, None, :], (2, blocks // 2 + 1, ROWS, LANES))
 
     def halves(matrix):
@@ -75,9 +76,36 @@
     return np.ascontiguousarray(twist), halves(forward), halves(inverse)
 
 
-def root(k, n):
+class Signed:
+    def __init__(self, value, minus=False):
+        self.value, self.minus = value, minus
+
+    def __neg__(self):
+        return Signed(self.value, not self.minus)
+
+    def __add__(self, other):
+        if self.minus == other.minus:
+            return Signed(self.value + other.value, self.minus)
+        first, second = (other, self) if self.minus else (self, other)
+        return Signed(first.value - second.value)
+
+    def __sub__(self, other):
+        return self + -other
+
+    def __mul__(self, factor):
+        return Signed(self.value * factor, self.minus)
+
+    def plain(self):
+        return -self.value if self.minus else self.value
+
+
+def turn(re, im, k, n):
+    if 8 * k == n:
+        c = math.sqrt(0.5)
+        return (re + im) * c, (im - re) * c
     angle = 2.0 * math.pi * k / n
-    return math.cos(angle), math.sin(angle)
+    c, s = math.cos(angle), math.sin(angle)
+    return re * c + im * s, im * c - re * s
 
 
 def real_fft(x):
@@ -91,11 +119,9 @@
     out[half] = (even[0][0] - odd[0][0], None)
     out[quarter] = (even[quarter][0], -odd[quarter][0])
     for k in range(1, quarter):
-        c, s = root(k, n)
-        re, im = odd[k]
-        t_re, t_im = re * c + im * s, im * c - re * s
-        out[k] = (even[k][0] + t_re, even[k][1] + t_im)
-        out[half - k] = (even[k][0] - t_re, t_im - even[k][1])
+        re, im = turn(*odd[k], k, n)
+        out[k] = (even[k][0] + re, even[k][1] + im)
+        out[half - k] = (even[k][0] - re, im - even[k][1])
     return out
 
 
@@ -107,14 +133,13 @@
     even, odd = [None] * (quarter + 1), [None] * (quarter + 1)
     even[0] = (w[0][0] + w[half][0], None)
     odd[0] = (w[0][0] - w[half][0], None)
-    even[quarter] = (2.0 * w[quarter][0], None)
-    odd[quarter] = (-2.0 * w[quarter][1], None)
+    even[quarter] = (w[quarter][0], None)
+    odd[quarter] = (-w[quarter][1], None)
     for k in range(1, quarter):
-        c, s = root(k, n)
         a, b = w[k], w[half - k]
         even[k] = (a[0] + b[0], a[1] - b[1])
-        re, im = a[0] - b[0], a[1] + b[1]
-        odd[k] = (re * c - im * s, im * c + re * s)
+        im, re = turn(a[1] + b[1], a[0] - b[0], k, n)
+        odd[k] = (re, im)
     x = [None] * n
     x[0::2], x[1::2] = real_ifft(even), real_ifft(odd)
     return x
@@ -158,26 +183,24 @@
     return pltpu.roll(after, LANES - 1, axis=1) - pltpu.roll(before, 1, axis=1)
 
 
-def pack_kernel(bands, blocks, x_ref, z_ref, c_ref, own_ref):
+def pack(rows, end, x_ref, out_ref):
+    edge, inner = end * (ROWS - 1), 1 + end * (ROWS - 3)
+    last = end == 1
+    half = jnp.where(last, rows.half[ROWS - 1 :], rows.half[:1])
+    weight = jnp.where(last, -rows.down[ROWS - 1 :], rows.up[:1])
+    for level in range(2):
+
+        def plane(field, row):
+            return x_ref[:, (field * 2 + level) * ROWS + row, :]
+
+        for k, field in enumerate((0, 2, 3)):
+            out_ref[k * 2 + level] = plane(field, edge)
+        out_ref[6 + level] = shifted_diff(plane(1, edge)) * half + weight * plane(2, inner)
+
+
+def pack_kernel(bands, x_ref, z_ref):
     rows = Rows(bands)
-
-    def plane(field, level, row):
-        return x_ref[pl.ds((field * 2 + level) * ROWS + row, blocks, stride=8 * ROWS), :]
-
-    for out, end in ((z_ref, rows.core), (c_ref, 1 - rows.core)):
-        edge, inner = end * (ROWS - 1), 1 + end * (ROWS - 3)
-        half, weight = (
-            jnp.where(end == 1, v[ROWS - 1 :], w[:1])
-            for v, w in ((rows.half, rows.half), (-rows.down, rows.up))
-        )
-        for level in range(2):
-            for k, field in enumerate((0, 2, 3)):
-                out[k * 2 + level] = plane(field, level, edge)
-            zonal, far = plane(1, level, edge), plane(2, level, inner)
-            out[6 + level] = shifted_diff(zonal) * half + weight * far
-    for side in range(2):
-        for level in range(2):
-            own_ref[side * 2 + level] = plane(2, level, side * (ROWS - 1))
+    pack(rows, rows.core, x_ref, z_ref)
 
 
 def parameters(rows, damp_ref, cutoff_ref, param_ref):
@@ -200,9 +223,15 @@
     return pl.ds(start if isinstance(start, int) else pl.multiple_of(start, ROWS), ROWS)
 
 
-def stencil_kernel(bands, blocks, x_ref, damp_ref, cutoff_ref, inc_ref, param_ref, mix_ref):
+def stencil_kernel(
+    bands, blocks, x_ref, damp_ref, cutoff_ref, inc_ref, param_ref, c_ref, own_ref, mix_ref
+):
     rows = Rows(bands)
     parameters(rows, damp_ref, cutoff_ref, param_ref)
+    pack(rows, 1 - rows.core, x_ref, c_ref)
+    for side in range(2):
+        for level in range(2):
+            own_ref[side * 2 + level] = x_ref[:, (4 + level) * ROWS + side * (ROWS - 1), :]
     row = lax.broadcasted_iota(jnp.int32, (ROWS, LANES), 0)
     up = jnp.where(row == ROWS - 1, 0.0, rows.up)
     down = jnp.where(row == 0, 0.0, rows.down)
@@ -224,7 +253,7 @@
         return pltpu.roll(here, 1, axis=0)
 
     def x(p, g):
-        return x_ref[tile(p, g), :]
+        return x_ref[p, pl.ds(g * ROWS, ROWS), :]
 
     def around(p):
         return lax.rem(p + blocks - 1, blocks), lax.rem(p + 1, blocks)
@@ -341,15 +370,18 @@
 
         def analyse(part):
             for i in range(width):
-                waves = real_fft([increment(p, part * width + i) for p in range(blocks)])
+                waves = real_fft([Signed(increment(p, part * width + i)) for p in range(blocks)])
                 at = slice(i * ROWS, (i + 1) * ROWS)
                 for k, (re, im) in enumerate(waves):
                     c, s = twist_ref[0, k], twist_ref[1, k]
-                    if im is None:
-                        turned = (re, jnp.zeros_like(re)) if k == 0 else (re * c, -(re * s))
+                    if k == 0:
+                        turned = re, Signed(jnp.zeros_like(re.value))
+                    elif im is None:
+                        turned = re * c, -(re * s)
                     else:
-                        turned = (re * c + im * s, im * c - re * s)
-                    wave_ref[part, k, at, :LANES], wave_ref[part, k, at, LANES:] = turned
+                        turned = re * c + im * s, im * c - re * s
+                    wave_ref[part, k, at, :LANES] = turned[0].plain()
+                    wave_ref[part, k, at, LANES:] = turned[1].plain()
 
         def product(values, table_ref):
             high, low = split(values)
@@ -375,7 +407,9 @@
                 at = slice(i * ROWS, (i + 1) * ROWS)
                 waves = []
                 for k in range(top + 1):
-                    re, im = wave_ref[part, k, at, :LANES], wave_ref[part, k, at, LANES:]
+                    re, im = (
+                        Signed(wave_ref[part, k, at, j : j + LANES]) for j in (0, LANES)
+                    )
                     c, s = twist_ref[0, k], twist_ref[1, k]
                     if k == 0:
                         waves.append((re, None))
@@ -384,6 +418,7 @@
                     else:
                         waves.append((re * c - im * s, im * c + re * s))
                 for p, smooth in enumerate(real_ifft(waves)):
+                    smooth = smooth.plain()
                     if not whole:
                         smooth = jnp.where(rows.polar, smooth, increment(p, g))
                     out_ref[tile(p, g), :] = x_ref[tile(p, g), :] + smooth
@@ -426,18 +461,13 @@
     )(state.reshape(fields, chips, 2, 2, ROWS, ncol))
     circles = lax.all_to_all(
         parts.reshape(blocks, -1, ncol), "lon", split_axis=0, concat_axis=0, tiled=True
-    ).reshape(-1, ncol)
+    )
 
     twist, forward, inverse = fourier_tables(blocks)
 
     plane = array(8, blocks, ncol)
-    z_mine, c_mine, own = call(
-        lambda *refs: pack_kernel(bands, blocks, *refs),
-        "pack",
-        (plane, plane, array(4, blocks, ncol)),
-        [vmem],
-        (vmem, vmem, vmem),
-        0,
+    z_mine = call(
+        lambda *refs: pack_kernel(bands, *refs), "pack", plane, [vmem], vmem, 0
     )(circles)
 
     swaps = []
@@ -446,21 +476,21 @@
             a, b = z * blocks + 2 * m + 1, (z + 1) * blocks + 2 * m
             swaps += [(a, b), (b, a)]
     z_other = lax.ppermute(z_mine, ("lat", "lon"), swaps)
-    pairs = [[2 * m, 2 * m + 1] for m in range(chips)]
-    c_both = lax.all_gather(c_mine, "lon", axis_index_groups=pairs)
-    increments, params = call(
+    increments, params, c_mine, own = call(
         lambda *refs: stencil_kernel(bands, blocks, *refs),
         "stencil",
-        (array(*circles.shape), array(3, ROWS, ncol)),
+        (array(blocks * 8 * ROWS, ncol), array(3, ROWS, ncol), plane, array(4, blocks, ncol)),
         [vmem] * 3,
-        (vmem, vmem),
+        (vmem,) * 4,
         2**28,
         [pltpu.VMEM((blocks, 2, ROWS, ncol), jnp.float32)],
     )(circles, damping, cutoff)
+    pairs = [[2 * m, 2 * m + 1] for m in range(chips)]
+    c_both = lax.all_gather(c_mine, "lon", axis_index_groups=pairs)
     moved = call(
         lambda *refs: filter_kernel(bands, blocks, *refs),
         "filter",
-        array(*circles.shape),
+        array(blocks * 8 * ROWS, ncol),
         [vmem] * 9,
         vmem,
         2**31,
@@ -468,7 +498,7 @@
             pltpu.VMEM((2, 10, blocks, ncol), jnp.float32),
             pltpu.VMEM((4, blocks // 2 + 1, 2 * ROWS, 2 * ncol), jnp.float32),
         ],
-    )(circles, increments, z_other, c_both, own, params, twist, forward, inverse)
+    )(circles.reshape(-1, ncol), increments, z_other, c_both, own, params, twist, forward, inverse)
 
     home = lax.all_to_all(
         moved.reshape(blocks, -1, ncol), "lon", split_axis=0, concat_axis=0, tiled=True

time: 58.9 us -> 58.6 us (level)
  transfers between devices with their start and end apart: 1 -> 1, of which waited for: 1 -> 1; matrix products, arithmetic and copies ran while one was open for 0% -> 0% of each run, Pallas kernels for 1% -> 2%
where the time goes in v5:
time: 58.6 us; the launch traced here: 58.4 us
  blocking collectives  49.6 us (85%)
  Pallas kernels  4.28 us (7%)
  starting transfers between devices  2.56 us (4%)
  local copies, waits for them, and re-layouts  1.25 us (2%)
  waiting for transfers between devices  0.65 us (1%)
    all_to_all x1, blocking collectives, on_device(): lax.all_to_all(parts.reshape(blocks, -1, ncol), 'lon', split_axis=0, conc...  26.8 us
    all_to_all x1, blocking collectives, on_device(): lax.all_to_all(moved.reshape(blocks, -1, ncol), 'lon', split_axis=0, conc...  20.6 us
    ppermute x1, starting transfers between devices, on_device(): z_other = lax.ppermute(z_mine, ('lat', 'lon'), swaps)  2.56 us
    all_gather x1, blocking collectives, on_device(): c_both = lax.all_gather(c_mine, 'lon', axis_index_groups=pairs)  2.13 us
    pallas_call x1, Pallas kernels, on_device(): call(lambda *refs: filter_kernel(bands, blocks, *refs), 'filter', array(b...  2.08 us
    unnamed x12, local copies, waits for them, and re-layouts  1.25 us
  transfers between devices with their start and end apart: 1, of which 1 were waited for; matrix products, arithmetic and copies ran while one was open for 0% of the time, Pallas kernels for 2%

profile of v5, /device:TPU:1, one launch (start us, length us, event | category | flops | bytes accessed | tf_op | source)
XLA Modules:
  0.0 58.4 jit_solution(6696784630735698827)
XLA Ops:
  0.0 0.0 copy-start
  0.0 1.2 %copy-done = f32[4,32,16,128]{3,2,1,0:T(8,128)S(1)} copy-done((f32[4,32,16,128]{3,2,1,0:T(8,128)S(1)}, f32[4,32,16,128]{3,2,1,0:T(8,128)}, u32[]{:S(2)}) %copy-start) | copy-done | bytes 1048600
  1.2 0.2 spread.1
  1.4 26.8 %all_to_all.10.refs_0_ = f32[32,64,128]{2,1,0:T(8,128)S(1)} all-to-all(f32[32,64,128]{2,1,0:T(8,128)S(1)} %bitcast.9), channel_id=1, replica_groups=mesh['lat'=16,'lon'=32] {'lon'}, dimensions={0} | all-to-all | bytes 2097152 | tf_op jit(solution)/shard_map/all_to_all | solution.py:462
  28.2 0.0 copy-start.1
  28.2 0.0 copy-start.2
  28.2 0.1 pack.1
  28.4 2.6 %collective-permute-start = (f32[8,32,128]{2,1,0:T(8,128)S(1)}, f32[8,32,128]{2,1,0:T(8,128)S(1)}, u32[]{:S(2)}, u32[]{:S(2)}) collective-permute-start(f32[8,32,128]{2,1,0:T(8,128)S(1)} %pack.1), channel_id=1, source_target_pairs={{1,32},{32,1},{3,34},{34,3},{5,36},{36,5},{7,38},{38,7},{9,40},{40... | collective-permute-start | bytes 393224 | tf_op jit(solution)/shard_map/ppermute | solution.py:478
  30.9 0.0 copy-done.1
  30.9 0.0 copy-done.2
  30.9 0.0 copy-start.4
  31.0 0.9 %stencil.1 = (f32[2048,128]{1,0:T(8,128)S(1)}, f32[3,8,128]{2,1,0:T(8,128)S(1)}, f32[8,32,128]{2,1,0:T(8,128)S(1)}, f32[4,32,128]{2,1,0:T(8,128)S(1)}) custom-call(f32[32,64,128]{2,1,0:T(8,128)S(1)} %all_to_all.10.refs_0_, f32[32]{0:T(128)S(1)} %copy-done.2, s32[256]{0:T(256)S(1)} %copy-done.1), custom_call_target="tpu_custom_call" | custom-call | flops 268435456 | bytes 4194304 | tf_op jit(solution)/shard_map/stencil/pallas_call | solution.py:479
  31.8 0.0 copy-start.3
  31.9 0.0 copy-start.5
  31.9 2.1 %all-gather = f32[16,32,128]{2,1,0:T(8,128)S(1)} all-gather(f32[8,32,128]{2,1,0:T(8,128)S(1)} %get-tuple-element.10), channel_id=2, replica_groups={{0,1},{2,3},{4,5},{6,7},{8,9},{10,11},{12,13},{14,15},{16,17},{18,19},{..., dimensions={0}, use_global_device_ids=true | all-gather | bytes 393216 | tf_op jit(solution)/shard_map/all_gather | solution.py:489
  34.0 0.6 %collective-permute-done.refs_2_ = f32[8,32,128]{2,1,0:T(8,128)S(1)} collective-permute-done((f32[8,32,128]{2,1,0:T(8,128)S(1)}, f32[8,32,128]{2,1,0:T(8,128)S(1)}, u32[]{:S(2)}, u32[]{:S(2)}) %collective-permute-start) | collective-permute-done | bytes 131104 | tf_op jit(solution)/shard_map/ppermute | solution.py:478
  34.6 0.0 copy-done.4
  34.7 0.0 copy-done.3
  34.7 0.0 copy-done.5
  34.7 2.1 %filter.1 = f32[2048,128]{1,0:T(8,128)S(1)} custom-call(f32[2048,128]{1,0:T(8,128)S(1)} %bitcast.7, f32[2048,128]{1,0:T(8,128)S(1)} %get-tuple-element.9.refs_1_, f32[8,32,128]{2,1,0:T(8,128)S(1)} %collective-permute-done.refs_2_, f32[2,8,32,128]{3,2,1,0:T(8,128)S(1)} %bitcast.12, f32[4,32,128]{2,1,0:T(8,128)S(1)} %get-tuple-element.11.refs_4_, ...), custom_call_target="tpu_custom_call" | custom-call | flops 2147483648 | bytes 4194304 | tf_op jit(solution)/shard_map/filter/pallas_call | solution.py:490
  36.8 20.6 %all_to_all.11 = f32[32,64,128]{2,1,0:T(8,128)S(1)} all-to-all(f32[32,64,128]{2,1,0:T(8,128)S(1)} %bitcast.11), channel_id=1, replica_groups=mesh['lat'=16,'lon'=32] {'lon'}, dimensions={0} | all-to-all | bytes 2097152 | tf_op jit(solution)/shard_map/all_to_all | solution.py:503
  57.4 1.0 %collect.1 = f32[4,16,2,2,8,128]{5,4,3,2,1,0:T(8,128)} custom-call(f32[16,2,4,2,8,128]{5,4,3,2,1,0:T(8,128)S(1)} %bitcast.8), custom_call_target="tpu_custom_call" | custom-call | bytes 4194304 | tf_op jit(solution)/shard_map/collect/pallas_call | solution.py:506
Async XLA Ops:
  0.0 1.2 %copy-start = (f32[4,32,16,128]{3,2,1,0:T(8,128)S(1)}, f32[4,32,16,128]{3,2,1,0:T(8,128)}, u32[]{:S(2)}) copy-start(f32[4,32,16,128]{3,2,1,0:T(8,128)} %param.6) | copy-start | bytes 3145732
  28.2 2.7 %copy-start.1 = (s32[256]{0:T(256)S(1)}, s32[256]{0:T(256)}, u32[]{:S(2)}) copy-start(s32[256]{0:T(256)} %refs_2_.1) | copy-start | bytes 3076
  28.2 2.7 %copy-start.2 = (f32[32]{0:T(128)S(1)}, f32[32]{0:T(128)}, u32[]{:S(2)}) copy-start(f32[32]{0:T(128)} %refs_1_.1) | copy-start | bytes 388
  28.4 6.3 %collective-permute-start = (f32[8,32,128]{2,1,0:T(8,128)S(1)}, f32[8,32,128]{2,1,0:T(8,128)S(1)}, u32[]{:S(2)}, u32[]{:S(2)}) collective-permute-start(f32[8,32,128]{2,1,0:T(8,128)S(1)} %pack.1), channel_id=1, source_target_pairs={{1,32},{32,1},{3,34},{34,3},{5,36},{36,5},{7,38},{38,7},{9,40},{40... | collective-permute-start | bytes 393224 | tf_op jit(solution)/shard_map/ppermute | solution.py:478
  30.9 3.7 %copy-start.4 = (bf16[2,256,256]{2,1,0:T(8,128)(2,1)S(1)}, bf16[2,256,256]{2,1,0:T(8,128)(2,1)}, u32[]{:S(2)}) copy-start(bf16[2,256,256]{2,1,0:T(8,128)(2,1)} %constant.7.clone.refs_7_) | copy-start | bytes 786436
  31.8 2.8 %copy-start.3 = (bf16[2,256,256]{2,1,0:T(8,128)(2,1)S(1)}, bf16[2,256,256]{2,1,0:T(8,128)(2,1)}, u32[]{:S(2)}) copy-start(bf16[2,256,256]{2,1,0:T(8,128)(2,1)} %constant.8.clone.refs_8_) | copy-start | bytes 786436
  31.9 2.8 %copy-start.5 = (f32[2,17,8,128]{3,2,1,0:T(8,128)S(1)}, f32[2,17,8,128]{3,2,1,0:T(8,128)}, u32[]{:S(2)}) copy-start(f32[2,17,8,128]{3,2,1,0:T(8,128)} %constant.6.clone.refs_6_) | copy-start | bytes 417796

commit v6 on v5

--- a/solution.py
+++ b/solution.py
@@ -145,13 +145,26 @@
     return x
 
 
-def spread_kernel(x_ref, out_ref, sems):
+def rank(lon, blocks):
+    return blocks - 1 - lon
+
+
+def spread_kernel(x_ref, out_ref):
+    fields, chips, levels, cores = x_ref.shape[:4]
+    for chip in range(chips):
+        for core in range(cores):
+            for field in range(fields):
+                for level in range(levels):
+                    out_ref[chip, core, field, level] = x_ref[field, chips - 1 - chip, level, core]
+
+
+def collect_kernel(x_ref, out_ref, sems):
     copies = []
     for field in range(4):
         for core in range(2):
             copies.append(
                 pltpu.make_async_copy(
-                    x_ref.at[field, :, :, core], out_ref.at[:, core, field], sems.at[field, core]
+                    x_ref.at[:, 1 - core, field], out_ref.at[field, :, :, core], sems.at[field, core]
                 )
             )
     for copy in copies:
@@ -160,21 +173,6 @@
         copy.wait()
 
 
-def collect_kernel(x_ref, out_ref, sems):
-    copies = []
-    for field in range(4):
-        for core in range(2):
-            copies.append(
-                pltpu.make_async_copy(
-                    x_ref.at[:, core, field], out_ref.at[field, :, :, core], sems.at[field, core]
-                )
-            )
-    for copy in copies:
-        copy.start()
-    for copy in copies:
-        copy.wait()
-
-
 def shifted_diff(here):
     blocks = here.shape[0]
     lane = lax.broadcasted_iota(jnp.int32, here.shape, 1)
@@ -204,7 +202,8 @@
 
 
 def parameters(rows, damp_ref, cutoff_ref, param_ref):
-    level = lax.axis_index("lon") // 2 * 2
+    blocks = lax.axis_size("lon")
+    level = rank(lax.axis_index("lon"), blocks) // 2 * 2
     damping = damp_ref[...].reshape(1, -1)
     at = lax.broadcasted_iota(jnp.int32, damping.shape, 1)
     for i in range(2):
@@ -362,7 +361,7 @@
     def _():
         for g in range(8):
             for p in range(blocks):
-                out_ref[tile(p, g), :] = x_ref[tile(p, g), :] + increment(p, g)
+                out_ref[tile(rank(p, blocks), g), :] = x_ref[tile(p, g), :] + increment(p, g)
 
     @pl.when(any_polar)
     def _():
@@ -421,7 +420,7 @@
                     smooth = smooth.plain()
                     if not whole:
                         smooth = jnp.where(rows.polar, smooth, increment(p, g))
-                    out_ref[tile(p, g), :] = x_ref[tile(p, g), :] + smooth
+                    out_ref[tile(rank(p, blocks), g), :] = x_ref[tile(p, g), :] + smooth
 
         parts = 8 // width
         for i in range(parts + 2):
@@ -457,7 +456,7 @@
 
     sems = [pltpu.SemaphoreType.DMA((fields, 2))]
     parts = call(
-        spread_kernel, "spread", array(chips, 2, fields, 2, ROWS, ncol), [hbm], vmem, 0, sems
+        spread_kernel, "spread", array(chips, 2, fields, 2, ROWS, ncol), [vmem], vmem, 0
     )(state.reshape(fields, chips, 2, 2, ROWS, ncol))
     circles = lax.all_to_all(
         parts.reshape(blocks, -1, ncol), "lon", split_axis=0, concat_axis=0, tiled=True
@@ -501,7 +500,12 @@
     )(circles.reshape(-1, ncol), increments, z_other, c_both, own, params, twist, forward, inverse)
 
     home = lax.all_to_all(
-        moved.reshape(blocks, -1, ncol), "lon", split_axis=0, concat_axis=0, tiled=True
+        moved.reshape(blocks, -1, ncol),
+        "lon",
+        split_axis=0,
+        concat_axis=0,
+        axis_index_groups=[[rank(lon, blocks) for lon in range(blocks)]],
+        tiled=True,
     )
     out = call(
         collect_kernel, "collect", array(fields, chips, 2, 2, ROWS, ncol), [vmem], hbm, 0, sems

time: 58.6 us -> 57.9 us (0.988)
  blocking collectives: 49.6 us -> 49 us
    all_to_all x1, blocking collectives: 20.6 us -> 20 us  [on_device(): lax.all_to_all(moved.reshape(blocks, -1, ncol), 'lon', split_axis=0, conc...]
where the time goes in v6:
time: 57.9 us; the launch traced here: 57.7 us
  blocking collectives  49 us (85%)
  Pallas kernels  4.19 us (7%)
  starting transfers between devices  2.56 us (4%)
  local copies, waits for them, and re-layouts  1.25 us (2%)
  waiting for transfers between devices  0.65 us (1%)
    all_to_all x1, blocking collectives, on_device(): lax.all_to_all(parts.reshape(blocks, -1, ncol), 'lon', split_axis=0, conc...  26.8 us
    all_to_all x1, blocking collectives, on_device(): lax.all_to_all(moved.reshape(blocks, -1, ncol), 'lon', split_axis=0, conc...  20 us
    ppermute x1, starting transfers between devices, on_device(): z_other = lax.ppermute(z_mine, ('lat', 'lon'), swaps)  2.56 us
    all_gather x1, blocking collectives, on_device(): c_both = lax.all_gather(c_mine, 'lon', axis_index_groups=pairs)  2.13 us
    pallas_call x1, Pallas kernels, on_device(): call(lambda *refs: filter_kernel(bands, blocks, *refs), 'filter', array(b...  2.08 us
    unnamed x12, local copies, waits for them, and re-layouts  1.25 us
  transfers between devices with their start and end apart: 1, of which 1 were waited for; matrix products, arithmetic and copies ran while one was open for 0% of the time, Pallas kernels for 2%

profile of v6, /device:TPU:1, one launch (start us, length us, event | category | flops | bytes accessed | tf_op | source)
XLA Modules:
  0.0 57.7 jit_solution(1758975800672618731)
XLA Ops:
  0.0 0.0 copy-start
  0.0 1.2 %copy-done = f32[4,32,16,128]{3,2,1,0:T(8,128)S(1)} copy-done((f32[4,32,16,128]{3,2,1,0:T(8,128)S(1)}, f32[4,32,16,128]{3,2,1,0:T(8,128)}, u32[]{:S(2)}) %copy-start) | copy-done | bytes 1048600
  1.2 0.1 spread.1
  1.3 26.8 %all_to_all.10.refs_0_ = f32[32,64,128]{2,1,0:T(8,128)S(1)} all-to-all(f32[32,64,128]{2,1,0:T(8,128)S(1)} %bitcast.9), channel_id=1, replica_groups=mesh['lat'=16,'lon'=32] {'lon'}, dimensions={0} | all-to-all | bytes 2097152 | tf_op jit(solution)/shard_map/all_to_all | solution.py:461
  28.1 0.0 copy-start.1
  28.1 0.0 copy-start.2
  28.1 0.1 pack.1
  28.3 2.6 %collective-permute-start = (f32[8,32,128]{2,1,0:T(8,128)S(1)}, f32[8,32,128]{2,1,0:T(8,128)S(1)}, u32[]{:S(2)}, u32[]{:S(2)}) collective-permute-start(f32[8,32,128]{2,1,0:T(8,128)S(1)} %pack.1), channel_id=1, source_target_pairs={{1,32},{32,1},{3,34},{34,3},{5,36},{36,5},{7,38},{38,7},{9,40},{40... | collective-permute-start | bytes 393224 | tf_op jit(solution)/shard_map/ppermute | solution.py:477
  30.8 0.0 copy-done.1
  30.8 0.0 copy-done.2
  30.8 0.0 copy-start.4
  30.9 0.9 %stencil.1 = (f32[2048,128]{1,0:T(8,128)S(1)}, f32[3,8,128]{2,1,0:T(8,128)S(1)}, f32[8,32,128]{2,1,0:T(8,128)S(1)}, f32[4,32,128]{2,1,0:T(8,128)S(1)}) custom-call(f32[32,64,128]{2,1,0:T(8,128)S(1)} %all_to_all.10.refs_0_, f32[32]{0:T(128)S(1)} %copy-done.2, s32[256]{0:T(256)S(1)} %copy-done.1), custom_call_target="tpu_custom_call" | custom-call | flops 268435456 | bytes 4194304 | tf_op jit(solution)/shard_map/stencil/pallas_call | solution.py:478
  31.7 0.0 copy-start.3
  31.8 0.0 copy-start.5
  31.8 2.1 %all-gather = f32[16,32,128]{2,1,0:T(8,128)S(1)} all-gather(f32[8,32,128]{2,1,0:T(8,128)S(1)} %get-tuple-element.10), channel_id=2, replica_groups={{0,1},{2,3},{4,5},{6,7},{8,9},{10,11},{12,13},{14,15},{16,17},{18,19},{..., dimensions={0}, use_global_device_ids=true | all-gather | bytes 393216 | tf_op jit(solution)/shard_map/all_gather | solution.py:488
  33.9 0.6 %collective-permute-done.refs_2_ = f32[8,32,128]{2,1,0:T(8,128)S(1)} collective-permute-done((f32[8,32,128]{2,1,0:T(8,128)S(1)}, f32[8,32,128]{2,1,0:T(8,128)S(1)}, u32[]{:S(2)}, u32[]{:S(2)}) %collective-permute-start) | collective-permute-done | bytes 131104 | tf_op jit(solution)/shard_map/ppermute | solution.py:477
  34.5 0.0 copy-done.4
  34.6 0.0 copy-done.3
  34.6 0.0 copy-done.5
  34.6 2.1 %filter.1 = f32[2048,128]{1,0:T(8,128)S(1)} custom-call(f32[2048,128]{1,0:T(8,128)S(1)} %bitcast.7, f32[2048,128]{1,0:T(8,128)S(1)} %get-tuple-element.9.refs_1_, f32[8,32,128]{2,1,0:T(8,128)S(1)} %collective-permute-done.refs_2_, f32[2,8,32,128]{3,2,1,0:T(8,128)S(1)} %bitcast.12, f32[4,32,128]{2,1,0:T(8,128)S(1)} %get-tuple-element.11.refs_4_, ...), custom_call_target="tpu_custom_call" | custom-call | flops 2147483648 | bytes 4194304 | tf_op jit(solution)/shard_map/filter/pallas_call | solution.py:489
  36.7 20.0 %all_to_all.11 = f32[32,64,128]{2,1,0:T(8,128)S(1)} all-to-all(f32[32,64,128]{2,1,0:T(8,128)S(1)} %bitcast.11), channel_id=1, replica_groups={{31,30,29,28,27,26,25,24,23,22,21,20,19,18,17,16,15,14,13,12,11,10,9,8,..., dimensions={0} | all-to-all | bytes 2097152 | tf_op jit(solution)/shard_map/all_to_all | solution.py:502
  56.7 1.0 %collect.1 = f32[4,16,2,2,8,128]{5,4,3,2,1,0:T(8,128)} custom-call(f32[16,2,4,2,8,128]{5,4,3,2,1,0:T(8,128)S(1)} %bitcast.8), custom_call_target="tpu_custom_call" | custom-call | bytes 4194304 | tf_op jit(solution)/shard_map/collect/pallas_call | solution.py:510
Async XLA Ops:
  0.0 1.2 %copy-start = (f32[4,32,16,128]{3,2,1,0:T(8,128)S(1)}, f32[4,32,16,128]{3,2,1,0:T(8,128)}, u32[]{:S(2)}) copy-start(f32[4,32,16,128]{3,2,1,0:T(8,128)} %param.6) | copy-start | bytes 3145732
  28.1 2.7 %copy-start.1 = (s32[256]{0:T(256)S(1)}, s32[256]{0:T(256)}, u32[]{:S(2)}) copy-start(s32[256]{0:T(256)} %refs_2_.1) | copy-start | bytes 3076
  28.1 2.7 %copy-start.2 = (f32[32]{0:T(128)S(1)}, f32[32]{0:T(128)}, u32[]{:S(2)}) copy-start(f32[32]{0:T(128)} %refs_1_.1) | copy-start | bytes 388
  28.3 6.3 %collective-permute-start = (f32[8,32,128]{2,1,0:T(8,128)S(1)}, f32[8,32,128]{2,1,0:T(8,128)S(1)}, u32[]{:S(2)}, u32[]{:S(2)}) collective-permute-start(f32[8,32,128]{2,1,0:T(8,128)S(1)} %pack.1), channel_id=1, source_target_pairs={{1,32},{32,1},{3,34},{34,3},{5,36},{36,5},{7,38},{38,7},{9,40},{40... | collective-permute-start | bytes 393224 | tf_op jit(solution)/shard_map/ppermute | solution.py:477
  30.8 3.7 %copy-start.4 = (bf16[2,256,256]{2,1,0:T(8,128)(2,1)S(1)}, bf16[2,256,256]{2,1,0:T(8,128)(2,1)}, u32[]{:S(2)}) copy-start(bf16[2,256,256]{2,1,0:T(8,128)(2,1)} %constant.7.clone.refs_7_) | copy-start | bytes 786436
  31.7 2.8 %copy-start.3 = (bf16[2,256,256]{2,1,0:T(8,128)(2,1)S(1)}, bf16[2,256,256]{2,1,0:T(8,128)(2,1)}, u32[]{:S(2)}) copy-start(bf16[2,256,256]{2,1,0:T(8,128)(2,1)} %constant.8.clone.refs_8_) | copy-start | bytes 786436
  31.8 2.8 %copy-start.5 = (f32[2,17,8,128]{3,2,1,0:T(8,128)S(1)}, f32[2,17,8,128]{3,2,1,0:T(8,128)}, u32[]{:S(2)}) copy-start(f32[2,17,8,128]{3,2,1,0:T(8,128)} %constant.6.clone.refs_6_) | copy-start | bytes 417796

commit v7 on v6

--- a/solution.py
+++ b/solution.py
@@ -145,8 +145,9 @@
     return x
 
 
-def rank(lon, blocks):
-    return blocks - 1 - lon
+def way_back(blocks):
+    first = blocks // 2 + blocks // 8 + 1
+    return [first] + [lon for lon in range(blocks - 1, -1, -1) if lon != first]
 
 
 def spread_kernel(x_ref, out_ref):
@@ -155,20 +156,27 @@
         for core in range(cores):
             for field in range(fields):
                 for level in range(levels):
-                    out_ref[chip, core, field, level] = x_ref[field, chips - 1 - chip, level, core]
-
-
-def collect_kernel(x_ref, out_ref, sems):
+                    out_ref[chip, core, field, level] = x_ref[field, chip, level, core]
+
+
+def collect_kernel(x_ref, out_ref, held_ref, sems):
+    fields, chips, levels, cores = out_ref.shape[:4]
+    order = way_back(chips * cores)
     copies = []
-    for field in range(4):
-        for core in range(2):
+    for field in range(fields):
+        for half in range(2):
+            part = pl.ds(half * chips // 2, chips // 2)
+            for chip in range(half * chips // 2, (half + 1) * chips // 2):
+                for core in range(cores):
+                    for level in range(levels):
+                        here = x_ref[order.index(chip * cores + core), field, level]
+                        held_ref[field, chip, level, core] = here
             copies.append(
                 pltpu.make_async_copy(
-                    x_ref.at[:, 1 - core, field], out_ref.at[field, :, :, core], sems.at[field, core]
+                    held_ref.at[field, part], out_ref.at[field, part], sems.at[field, half]
                 )
             )
-    for copy in copies:
-        copy.start()
+            copies[-1].start()
     for copy in copies:
         copy.wait()
 
@@ -202,8 +210,7 @@
 
 
 def parameters(rows, damp_ref, cutoff_ref, param_ref):
-    blocks = lax.axis_size("lon")
-    level = rank(lax.axis_index("lon"), blocks) // 2 * 2
+    level = lax.axis_index("lon") // 2 * 2
     damping = damp_ref[...].reshape(1, -1)
     at = lax.broadcasted_iota(jnp.int32, damping.shape, 1)
     for i in range(2):
@@ -340,6 +347,7 @@
             more_ref[side, 8 + level] = step * damp_inner * extra
 
     row = lax.broadcasted_iota(jnp.int32, (ROWS, LANES), 0)
+    order = way_back(blocks)
 
     def increment(p, g):
         def more(side, k):
@@ -361,7 +369,7 @@
     def _():
         for g in range(8):
             for p in range(blocks):
-                out_ref[tile(rank(p, blocks), g), :] = x_ref[tile(p, g), :] + increment(p, g)
+                out_ref[tile(order.index(p), g), :] = x_ref[tile(p, g), :] + increment(p, g)
 
     @pl.when(any_polar)
     def _():
@@ -420,7 +428,7 @@
                     smooth = smooth.plain()
                     if not whole:
                         smooth = jnp.where(rows.polar, smooth, increment(p, g))
-                    out_ref[tile(rank(p, blocks), g), :] = x_ref[tile(p, g), :] + smooth
+                    out_ref[tile(order.index(p), g), :] = x_ref[tile(p, g), :] + smooth
 
         parts = 8 // width
         for i in range(parts + 2):
@@ -454,7 +462,6 @@
     def array(*shape):
         return jax.ShapeDtypeStruct(shape, jnp.float32)
 
-    sems = [pltpu.SemaphoreType.DMA((fields, 2))]
     parts = call(
         spread_kernel, "spread", array(chips, 2, fields, 2, ROWS, ncol), [vmem], vmem, 0
     )(state.reshape(fields, chips, 2, 2, ROWS, ncol))
@@ -504,12 +511,19 @@
         "lon",
         split_axis=0,
         concat_axis=0,
-        axis_index_groups=[[rank(lon, blocks) for lon in range(blocks)]],
+        axis_index_groups=[way_back(blocks)],
         tiled=True,
     )
+    whole = (fields, chips, 2, 2, ROWS, ncol)
     out = call(
-        collect_kernel, "collect", array(fields, chips, 2, 2, ROWS, ncol), [vmem], hbm, 0, sems
-    )(home.reshape(chips, 2, fields, 2, ROWS, ncol))
+        collect_kernel,
+        "collect",
+        array(*whole),
+        [vmem],
+        hbm,
+        0,
+        [pltpu.VMEM(whole, jnp.float32), pltpu.SemaphoreType.DMA((fields, 2))],
+    )(home.reshape(blocks, fields, 2, ROWS, ncol))
     return out.reshape(state.shape)
 
 

time: 57.9 us -> 57.4 us (level)
  no operation moved by 1% of the time
where the time goes in v7:
time: 57.4 us; the launch traced here: 57.2 us
  blocking collectives  48.5 us (84%)
  Pallas kernels  4.2 us (7%)
  starting transfers between devices  2.56 us (4%)
  local copies, waits for them, and re-layouts  1.25 us (2%)
  waiting for transfers between devices  0.65 us (1%)
    all_to_all x1, blocking collectives, on_device(): lax.all_to_all(parts.reshape(blocks, -1, ncol), 'lon', split_axis=0, conc...  26.8 us
    all_to_all x1, blocking collectives, on_device(): lax.all_to_all(moved.reshape(blocks, -1, ncol), 'lon', split_axis=0, conc...  19.5 us
    ppermute x1, starting transfers between devices, on_device(): z_other = lax.ppermute(z_mine, ('lat', 'lon'), swaps)  2.56 us
    all_gather x1, blocking collectives, on_device(): c_both = lax.all_gather(c_mine, 'lon', axis_index_groups=pairs)  2.13 us
    pallas_call x1, Pallas kernels, on_device(): call(lambda *refs: filter_kernel(bands, blocks, *refs), 'filter', array(b...  2.08 us
    unnamed x12, local copies, waits for them, and re-layouts  1.25 us
  transfers between devices with their start and end apart: 1, of which 1 were waited for; matrix products, arithmetic and copies ran while one was open for 0% of the time, Pallas kernels for 2%

profile of v7, /device:TPU:1, one launch (start us, length us, event | category | flops | bytes accessed | tf_op | source)
XLA Modules:
  0.0 57.2 jit_solution(2443581091779859179)
XLA Ops:
  0.0 0.0 copy-start
  0.0 1.2 %copy-done = f32[4,32,16,128]{3,2,1,0:T(8,128)S(1)} copy-done((f32[4,32,16,128]{3,2,1,0:T(8,128)S(1)}, f32[4,32,16,128]{3,2,1,0:T(8,128)}, u32[]{:S(2)}) %copy-start) | copy-done | bytes 1048600
  1.2 0.1 spread.1
  1.3 26.8 %all_to_all.10.refs_0_ = f32[32,64,128]{2,1,0:T(8,128)S(1)} all-to-all(f32[32,64,128]{2,1,0:T(8,128)S(1)} %bitcast.9), channel_id=1, replica_groups=mesh['lat'=16,'lon'=32] {'lon'}, dimensions={0} | all-to-all | bytes 2097152 | tf_op jit(solution)/shard_map/all_to_all | solution.py:468
  28.1 0.0 copy-start.1
  28.1 0.0 copy-start.2
  28.1 0.1 pack.1
  28.3 2.6 %collective-permute-start = (f32[8,32,128]{2,1,0:T(8,128)S(1)}, f32[8,32,128]{2,1,0:T(8,128)S(1)}, u32[]{:S(2)}, u32[]{:S(2)}) collective-permute-start(f32[8,32,128]{2,1,0:T(8,128)S(1)} %pack.1), channel_id=1, source_target_pairs={{1,32},{32,1},{3,34},{34,3},{5,36},{36,5},{7,38},{38,7},{9,40},{40... | collective-permute-start | bytes 393224 | tf_op jit(solution)/shard_map/ppermute | solution.py:484
  30.8 0.0 copy-done.1
  30.8 0.0 copy-done.2
  30.8 0.0 copy-start.4
  30.9 0.9 %stencil.1 = (f32[2048,128]{1,0:T(8,128)S(1)}, f32[3,8,128]{2,1,0:T(8,128)S(1)}, f32[8,32,128]{2,1,0:T(8,128)S(1)}, f32[4,32,128]{2,1,0:T(8,128)S(1)}) custom-call(f32[32,64,128]{2,1,0:T(8,128)S(1)} %all_to_all.10.refs_0_, f32[32]{0:T(128)S(1)} %copy-done.2, s32[256]{0:T(256)S(1)} %copy-done.1), custom_call_target="tpu_custom_call" | custom-call | flops 268435456 | bytes 4194304 | tf_op jit(solution)/shard_map/stencil/pallas_call | solution.py:485
  31.7 0.0 copy-start.3
  31.8 0.0 copy-start.5
  31.8 2.1 %all-gather = f32[16,32,128]{2,1,0:T(8,128)S(1)} all-gather(f32[8,32,128]{2,1,0:T(8,128)S(1)} %get-tuple-element.10), channel_id=2, replica_groups={{0,1},{2,3},{4,5},{6,7},{8,9},{10,11},{12,13},{14,15},{16,17},{18,19},{..., dimensions={0}, use_global_device_ids=true | all-gather | bytes 393216 | tf_op jit(solution)/shard_map/all_gather | solution.py:495
  33.9 0.6 %collective-permute-done.refs_2_ = f32[8,32,128]{2,1,0:T(8,128)S(1)} collective-permute-done((f32[8,32,128]{2,1,0:T(8,128)S(1)}, f32[8,32,128]{2,1,0:T(8,128)S(1)}, u32[]{:S(2)}, u32[]{:S(2)}) %collective-permute-start) | collective-permute-done | bytes 131104 | tf_op jit(solution)/shard_map/ppermute | solution.py:484
  34.5 0.0 copy-done.4
  34.6 0.0 copy-done.3
  34.6 0.0 copy-done.5
  34.6 2.1 %filter.1 = f32[2048,128]{1,0:T(8,128)S(1)} custom-call(f32[2048,128]{1,0:T(8,128)S(1)} %bitcast.7, f32[2048,128]{1,0:T(8,128)S(1)} %get-tuple-element.9.refs_1_, f32[8,32,128]{2,1,0:T(8,128)S(1)} %collective-permute-done.refs_2_, f32[2,8,32,128]{3,2,1,0:T(8,128)S(1)} %bitcast.12, f32[4,32,128]{2,1,0:T(8,128)S(1)} %get-tuple-element.11.refs_4_, ...), custom_call_target="tpu_custom_call" | custom-call | flops 2147483648 | bytes 4194304 | tf_op jit(solution)/shard_map/filter/pallas_call | solution.py:496
  36.7 19.5 %all_to_all.11 = f32[32,64,128]{2,1,0:T(8,128)S(1)} all-to-all(f32[32,64,128]{2,1,0:T(8,128)S(1)} %bitcast.11), channel_id=1, replica_groups={{21,31,30,29,28,27,26,25,24,23,22,20,19,18,17,16,15,14,13,12,11,10,9,8,..., dimensions={0} | all-to-all | bytes 2097152 | tf_op jit(solution)/shard_map/all_to_all | solution.py:509
  56.2 1.0 %collect.1 = f32[4,16,2,2,8,128]{5,4,3,2,1,0:T(8,128)} custom-call(f32[32,4,2,8,128]{4,3,2,1,0:T(8,128)S(1)} %bitcast.8), custom_call_target="tpu_custom_call" | custom-call | bytes 4194304 | tf_op jit(solution)/shard_map/collect/pallas_call | solution.py:518
Async XLA Ops:
  0.0 1.2 %copy-start = (f32[4,32,16,128]{3,2,1,0:T(8,128)S(1)}, f32[4,32,16,128]{3,2,1,0:T(8,128)}, u32[]{:S(2)}) copy-start(f32[4,32,16,128]{3,2,1,0:T(8,128)} %param.6) | copy-start | bytes 3145732
  28.1 2.7 %copy-start.1 = (s32[256]{0:T(256)S(1)}, s32[256]{0:T(256)}, u32[]{:S(2)}) copy-start(s32[256]{0:T(256)} %refs_2_.1) | copy-start | bytes 3076
  28.1 2.7 %copy-start.2 = (f32[32]{0:T(128)S(1)}, f32[32]{0:T(128)}, u32[]{:S(2)}) copy-start(f32[32]{0:T(128)} %refs_1_.1) | copy-start | bytes 388
  28.3 6.3 %collective-permute-start = (f32[8,32,128]{2,1,0:T(8,128)S(1)}, f32[8,32,128]{2,1,0:T(8,128)S(1)}, u32[]{:S(2)}, u32[]{:S(2)}) collective-permute-start(f32[8,32,128]{2,1,0:T(8,128)S(1)} %pack.1), channel_id=1, source_target_pairs={{1,32},{32,1},{3,34},{34,3},{5,36},{36,5},{7,38},{38,7},{9,40},{40... | collective-permute-start | bytes 393224 | tf_op jit(solution)/shard_map/ppermute | solution.py:484
  30.8 3.7 %copy-start.4 = (bf16[2,256,256]{2,1,0:T(8,128)(2,1)S(1)}, bf16[2,256,256]{2,1,0:T(8,128)(2,1)}, u32[]{:S(2)}) copy-start(bf16[2,256,256]{2,1,0:T(8,128)(2,1)} %constant.7.clone.refs_7_) | copy-start | bytes 786436
  31.7 2.8 %copy-start.3 = (bf16[2,256,256]{2,1,0:T(8,128)(2,1)S(1)}, bf16[2,256,256]{2,1,0:T(8,128)(2,1)}, u32[]{:S(2)}) copy-start(bf16[2,256,256]{2,1,0:T(8,128)(2,1)} %constant.8.clone.refs_8_) | copy-start | bytes 786436
  31.8 2.8 %copy-start.5 = (f32[2,17,8,128]{3,2,1,0:T(8,128)S(1)}, f32[2,17,8,128]{3,2,1,0:T(8,128)}, u32[]{:S(2)}) copy-start(f32[2,17,8,128]{3,2,1,0:T(8,128)} %constant.6.clone.refs_6_) | copy-start | bytes 417796

commit v8 on v7

--- a/solution.py
+++ b/solution.py
@@ -147,7 +147,7 @@
 
 def way_back(blocks):
     first = blocks // 2 + blocks // 8 + 1
-    return [first] + [lon for lon in range(blocks - 1, -1, -1) if lon != first]
+    return [first] + [lon for lon in range(blocks) if lon != first]
 
 
 def spread_kernel(x_ref, out_ref):

time: 57.4 us -> 57 us (level)
  blocking collectives: 48.5 us -> 47.8 us
    all_to_all x1, blocking collectives: 19.5 us -> 18.9 us  [on_device(): lax.all_to_all(moved.reshape(blocks, -1, ncol), 'lon', split_axis=0, conc...]
where the time goes in v8:
time: 57 us; the launch traced here: 56.6 us
  blocking collectives  47.8 us (84%)
  Pallas kernels  4.2 us (7%)
  starting transfers between devices  2.56 us (4%)
  local copies, waits for them, and re-layouts  1.25 us (2%)
  waiting for transfers between devices  0.65 us (1%)
    all_to_all x1, blocking collectives, on_device(): lax.all_to_all(parts.reshape(blocks, -1, ncol), 'lon', split_axis=0, conc...  26.8 us
    all_to_all x1, blocking collectives, on_device(): lax.all_to_all(moved.reshape(blocks, -1, ncol), 'lon', split_axis=0, conc...  18.9 us
    ppermute x1, starting transfers between devices, on_device(): z_other = lax.ppermute(z_mine, ('lat', 'lon'), swaps)  2.56 us
    all_gather x1, blocking collectives, on_device(): c_both = lax.all_gather(c_mine, 'lon', axis_index_groups=pairs)  2.13 us
    pallas_call x1, Pallas kernels, on_device(): call(lambda *refs: filter_kernel(bands, blocks, *refs), 'filter', array(b...  2.08 us
    unnamed x12, local copies, waits for them, and re-layouts  1.25 us
  transfers between devices with their start and end apart: 1, of which 1 were waited for; matrix products, arithmetic and copies ran while one was open for 0% of the time, Pallas kernels for 2%

profile of v8, /device:TPU:1, one launch (start us, length us, event | category | flops | bytes accessed | tf_op | source)
XLA Modules:
  0.0 56.6 jit_solution(14695291551428128520)
XLA Ops:
  0.0 0.0 copy-start
  0.0 1.2 %copy-done = f32[4,32,16,128]{3,2,1,0:T(8,128)S(1)} copy-done((f32[4,32,16,128]{3,2,1,0:T(8,128)S(1)}, f32[4,32,16,128]{3,2,1,0:T(8,128)}, u32[]{:S(2)}) %copy-start) | copy-done | bytes 1048600
  1.2 0.1 spread.1
  1.3 26.8 %all_to_all.10.refs_0_ = f32[32,64,128]{2,1,0:T(8,128)S(1)} all-to-all(f32[32,64,128]{2,1,0:T(8,128)S(1)} %bitcast.9), channel_id=1, replica_groups=mesh['lat'=16,'lon'=32] {'lon'}, dimensions={0} | all-to-all | bytes 2097152 | tf_op jit(solution)/shard_map/all_to_all | solution.py:468
  28.1 0.0 copy-start.1
  28.1 0.0 copy-start.2
  28.1 0.1 pack.1
  28.3 2.6 %collective-permute-start = (f32[8,32,128]{2,1,0:T(8,128)S(1)}, f32[8,32,128]{2,1,0:T(8,128)S(1)}, u32[]{:S(2)}, u32[]{:S(2)}) collective-permute-start(f32[8,32,128]{2,1,0:T(8,128)S(1)} %pack.1), channel_id=1, source_target_pairs={{1,32},{32,1},{3,34},{34,3},{5,36},{36,5},{7,38},{38,7},{9,40},{40... | collective-permute-start | bytes 393224 | tf_op jit(solution)/shard_map/ppermute | solution.py:484
  30.8 0.0 copy-done.1
  30.8 0.0 copy-done.2
  30.8 0.0 copy-start.4
  30.9 0.9 %stencil.1 = (f32[2048,128]{1,0:T(8,128)S(1)}, f32[3,8,128]{2,1,0:T(8,128)S(1)}, f32[8,32,128]{2,1,0:T(8,128)S(1)}, f32[4,32,128]{2,1,0:T(8,128)S(1)}) custom-call(f32[32,64,128]{2,1,0:T(8,128)S(1)} %all_to_all.10.refs_0_, f32[32]{0:T(128)S(1)} %copy-done.2, s32[256]{0:T(256)S(1)} %copy-done.1), custom_call_target="tpu_custom_call" | custom-call | flops 268435456 | bytes 4194304 | tf_op jit(solution)/shard_map/stencil/pallas_call | solution.py:485
  31.7 0.0 copy-start.3
  31.8 0.0 copy-start.5
  31.8 2.1 %all-gather = f32[16,32,128]{2,1,0:T(8,128)S(1)} all-gather(f32[8,32,128]{2,1,0:T(8,128)S(1)} %get-tuple-element.10), channel_id=2, replica_groups={{0,1},{2,3},{4,5},{6,7},{8,9},{10,11},{12,13},{14,15},{16,17},{18,19},{..., dimensions={0}, use_global_device_ids=true | all-gather | bytes 393216 | tf_op jit(solution)/shard_map/all_gather | solution.py:495
  33.9 0.6 %collective-permute-done.refs_2_ = f32[8,32,128]{2,1,0:T(8,128)S(1)} collective-permute-done((f32[8,32,128]{2,1,0:T(8,128)S(1)}, f32[8,32,128]{2,1,0:T(8,128)S(1)}, u32[]{:S(2)}, u32[]{:S(2)}) %collective-permute-start) | collective-permute-done | bytes 131104 | tf_op jit(solution)/shard_map/ppermute | solution.py:484
  34.5 0.0 copy-done.4
  34.6 0.0 copy-done.3
  34.6 0.0 copy-done.5
  34.6 2.1 %filter.1 = f32[2048,128]{1,0:T(8,128)S(1)} custom-call(f32[2048,128]{1,0:T(8,128)S(1)} %bitcast.7, f32[2048,128]{1,0:T(8,128)S(1)} %get-tuple-element.9.refs_1_, f32[8,32,128]{2,1,0:T(8,128)S(1)} %collective-permute-done.refs_2_, f32[2,8,32,128]{3,2,1,0:T(8,128)S(1)} %bitcast.12, f32[4,32,128]{2,1,0:T(8,128)S(1)} %get-tuple-element.11.refs_4_, ...), custom_call_target="tpu_custom_call" | custom-call | flops 2147483648 | bytes 4194304 | tf_op jit(solution)/shard_map/filter/pallas_call | solution.py:496
  36.7 18.9 %all_to_all.11 = f32[32,64,128]{2,1,0:T(8,128)S(1)} all-to-all(f32[32,64,128]{2,1,0:T(8,128)S(1)} %bitcast.11), channel_id=1, replica_groups={{21,0,1,2,3,4,5,6,7,8,9,10,11,12,13,14,15,16,17,18,19,20,22,23,24,25,26..., dimensions={0} | all-to-all | bytes 2097152 | tf_op jit(solution)/shard_map/all_to_all | solution.py:509
  55.5 1.0 %collect.1 = f32[4,16,2,2,8,128]{5,4,3,2,1,0:T(8,128)} custom-call(f32[32,4,2,8,128]{4,3,2,1,0:T(8,128)S(1)} %bitcast.8), custom_call_target="tpu_custom_call" | custom-call | bytes 4194304 | tf_op jit(solution)/shard_map/collect/pallas_call | solution.py:518
Async XLA Ops:
  0.0 1.2 %copy-start = (f32[4,32,16,128]{3,2,1,0:T(8,128)S(1)}, f32[4,32,16,128]{3,2,1,0:T(8,128)}, u32[]{:S(2)}) copy-start(f32[4,32,16,128]{3,2,1,0:T(8,128)} %param.6) | copy-start | bytes 3145732
  28.1 2.7 %copy-start.1 = (s32[256]{0:T(256)S(1)}, s32[256]{0:T(256)}, u32[]{:S(2)}) copy-start(s32[256]{0:T(256)} %refs_2_.1) | copy-start | bytes 3076
  28.1 2.7 %copy-start.2 = (f32[32]{0:T(128)S(1)}, f32[32]{0:T(128)}, u32[]{:S(2)}) copy-start(f32[32]{0:T(128)} %refs_1_.1) | copy-start | bytes 388
  28.3 6.3 %collective-permute-start = (f32[8,32,128]{2,1,0:T(8,128)S(1)}, f32[8,32,128]{2,1,0:T(8,128)S(1)}, u32[]{:S(2)}, u32[]{:S(2)}) collective-permute-start(f32[8,32,128]{2,1,0:T(8,128)S(1)} %pack.1), channel_id=1, source_target_pairs={{1,32},{32,1},{3,34},{34,3},{5,36},{36,5},{7,38},{38,7},{9,40},{40... | collective-permute-start | bytes 393224 | tf_op jit(solution)/shard_map/ppermute | solution.py:484
  30.8 3.7 %copy-start.4 = (bf16[2,256,256]{2,1,0:T(8,128)(2,1)S(1)}, bf16[2,256,256]{2,1,0:T(8,128)(2,1)}, u32[]{:S(2)}) copy-start(bf16[2,256,256]{2,1,0:T(8,128)(2,1)} %constant.7.clone.refs_7_) | copy-start | bytes 786436
  31.7 2.8 %copy-start.3 = (bf16[2,256,256]{2,1,0:T(8,128)(2,1)S(1)}, bf16[2,256,256]{2,1,0:T(8,128)(2,1)}, u32[]{:S(2)}) copy-start(bf16[2,256,256]{2,1,0:T(8,128)(2,1)} %constant.8.clone.refs_8_) | copy-start | bytes 786436
  31.8 2.8 %copy-start.5 = (f32[2,17,8,128]{3,2,1,0:T(8,128)S(1)}, f32[2,17,8,128]{3,2,1,0:T(8,128)}, u32[]{:S(2)}) copy-start(f32[2,17,8,128]{3,2,1,0:T(8,128)} %constant.6.clone.refs_6_) | copy-start | bytes 417796
